TPU v7x, 32 devices: a whole 2x2x4 slice. The times are simulated.
32 devices in a mesh: angle: 4 (over z), slab: 4 (over x, core), tile: 2 (over y).
Axes of the slice: x: 2, y: 2, z: 4, core: 2. Of those that a mesh axis runs over, the one named last changes fastest.
Arguments:
- volume: bfloat16 [2, 4, 384, 1536], P(None, 'slab', 'tile'), may hold values from -2 to 2
- probe_wave: float32 [2, 256, 256], replicated, may hold values from -6 to 6
- amplitudes: bfloat16 [4, 2, 4, 2, 256, 256], P('angle', 'tile', 'slab'), may hold values from 0.099609375 to 3
- offsets: int32 [4, 2, 4, 2], P('angle', 'tile', 'slab'), may hold values from 0 to 128
- column_starts: int32 [4, 2, 4, 2], P('angle', 'tile', 'slab'), may hold values from 0 to 1280
- counts: int32 [4, 2, 4], P('angle', 'tile', 'slab'), may hold values from 1 to 2, as said below
- angle_ids: int32 [4], P('angle'), may hold values from 0 to 1199
Outputs:
- new_volume: float32 [2, 4, 384, 1536], P(None, 'slab', 'tile')
Inputs may be any that keep to these rules, and one draw needn't show every extreme that they name: counts gives the live slots of one device; slots at or beyond it are ignored; in every draw some device has 2.
All inputs are finite; a program needn't handle non-finite values.
Results may differ from a plain program's by a relative error of at most 0.04.
Values may be sent and summed in bfloat16 or wider, within the bound.
A program may use at most 64 MiB of HBM per device.

v0:
```python
import jax
import jax.numpy as jnp
from jax import lax
from jax.sharding import PartitionSpec as P

angle_center = 600
shear_divisor = 64
step_size = 0.03
floor_square = 0.25


def passed_along(value, axis, steps):
    count = lax.axis_size(axis)
    initial, last = (max(0, -steps), min(count, count - steps))
    return lax.ppermute(value, axis, [(source, source + steps) for source in range(initial, last)])


def dft_tables(plane_width):
    index_line = jnp.arange(plane_width, dtype=jnp.int32)
    product_mod = jnp.mod(index_line[:, None] * index_line[None, :], plane_width)
    phase_table = product_mod.astype(jnp.float32) * (2.0 * 3.141592653589793 / plane_width)
    scale_factor = plane_width ** (-0.5)
    table_real = (jnp.cos(phase_table) * scale_factor).astype(jnp.bfloat16)
    table_imag = (-jnp.sin(phase_table) * scale_factor).astype(jnp.bfloat16)
    return (table_real, table_imag)


def shear_shifts(angle_value, first_layer, layer_count, total_depth, column_count):
    layer_index = first_layer + jnp.arange(layer_count, dtype=jnp.int32)
    offset_layer = layer_index - total_depth // 2
    sheared = jnp.floor_divide((angle_value - angle_center) * offset_layer, shear_divisor)
    return jnp.mod(sheared, column_count)


def roll_columns(field, amount):
    return jnp.roll(field, amount, axis=-1)


def twodot(left_matrix, right_matrix):
    return jnp.dot(left_matrix, right_matrix, preferred_element_type=jnp.float32)


def patch_gradient(window, probe_wave, pattern, table_real, table_imag):
    window_wide = window.astype(jnp.float32)
    trans_mag = jnp.exp(-window_wide[1])
    trans_real = trans_mag * jnp.cos(window_wide[0])
    trans_imag = trans_mag * jnp.sin(window_wide[0])
    wave_real = (probe_wave[0] * trans_real - probe_wave[1] * trans_imag).astype(jnp.bfloat16)
    wave_imag = (probe_wave[0] * trans_imag + probe_wave[1] * trans_real).astype(jnp.bfloat16)
    left_real = (twodot(table_real, wave_real) - twodot(table_imag, wave_imag)).astype(jnp.bfloat16)
    left_imag = (twodot(table_real, wave_imag) + twodot(table_imag, wave_real)).astype(jnp.bfloat16)
    far_real = twodot(left_real, table_real) - twodot(left_imag, table_imag)
    far_imag = twodot(left_real, table_imag) + twodot(left_imag, table_real)
    ratio = pattern.astype(jnp.float32) / jnp.sqrt(
        far_real * far_real + far_imag * far_imag + floor_square
    )
    keeping = 1.0 - ratio
    resid_real = (far_real * keeping).astype(jnp.bfloat16)
    resid_imag = (far_imag * keeping).astype(jnp.bfloat16)
    back_real = (twodot(table_real, resid_real) + twodot(table_imag, resid_imag)).astype(
        jnp.bfloat16
    )
    back_imag = (twodot(table_real, resid_imag) - twodot(table_imag, resid_real)).astype(
        jnp.bfloat16
    )
    exit_real = twodot(back_real, table_real) + twodot(back_imag, table_imag)
    exit_imag = twodot(back_imag, table_real) - twodot(back_real, table_imag)
    mixed_real = probe_wave[0] * exit_real + probe_wave[1] * exit_imag
    mixed_imag = probe_wave[0] * exit_imag - probe_wave[1] * exit_real
    final_real = trans_real * mixed_real + trans_imag * mixed_imag
    final_imag = trans_real * mixed_imag - trans_imag * mixed_real
    return jnp.stack([final_imag, -final_real])


def slot_update(
    buffer, extended, start_row, start_column, pattern, probe_wave, table_real, table_imag
):
    plane_width = pattern.shape[-1]
    zero_index = jnp.zeros((), jnp.int32)
    corner = (zero_index, start_row, start_column)
    window = lax.dynamic_slice(extended, corner, (2, plane_width, plane_width))
    gradient = patch_gradient(window, probe_wave, pattern, table_real, table_imag)
    previous = lax.dynamic_slice(buffer, corner, (2, plane_width, plane_width))
    return lax.dynamic_update_slice(buffer, previous + gradient, corner)


def per_device(volume, probe_wave, amplitudes, offsets, column_starts, counts, angle_ids):
    layer_count = volume.shape[1]
    tile_rows = volume.shape[2]
    column_count = volume.shape[3]
    plane_width = amplitudes.shape[-1]
    capacity = offsets.shape[3]
    slab_total = lax.axis_size("slab")
    slab_number = lax.axis_index("slab")
    table_real, table_imag = dft_tables(plane_width)
    shifts = shear_shifts(
        angle_ids[0], slab_number * layer_count, layer_count, layer_count * slab_total, column_count
    )
    rolled = jax.vmap(roll_columns, in_axes=(1, 0))(volume, -shifts)
    partial_sum = jnp.sum(rolled.astype(jnp.float32), axis=0)
    projection = lax.psum(partial_sum.astype(jnp.bfloat16), "slab")
    rows_after = passed_along(projection, "tile", -1)
    extended = jnp.concatenate([projection, rows_after], axis=1)
    own_patterns = amplitudes.reshape(capacity, plane_width, plane_width)
    own_starts = offsets.reshape(capacity)
    own_columns = column_starts.reshape(capacity)
    own_count = counts.reshape(1)
    zero_buffer = jnp.zeros(extended.shape, jnp.float32)

    def visit_own(position, current):
        return slot_update(
            current,
            extended,
            own_starts[position],
            own_columns[position],
            own_patterns[position],
            probe_wave,
            table_real,
            table_imag,
        )

    buffer = lax.fori_loop(0, own_count[0], visit_own, zero_buffer)
    spilled = passed_along(buffer[:, tile_rows:].astype(jnp.bfloat16), "tile", 1).astype(
        jnp.float32
    )
    tile_gradient = buffer[:, :tile_rows] + spilled
    plane_gradient = lax.psum(tile_gradient.astype(jnp.bfloat16), "slab").astype(jnp.float32)
    layer_gradient = jnp.moveaxis(
        jax.vmap(roll_columns, in_axes=(None, 0))(plane_gradient, shifts), 0, 1
    )
    summed_gradient = lax.psum(layer_gradient.astype(jnp.bfloat16), "angle").astype(jnp.float32)
    return volume.astype(jnp.float32) - step_size * summed_gradient


def solution(mesh):
    in_specs = (
        P(None, "slab", "tile", None),
        P(),
        P("angle", "tile", "slab", None, None, None),
        P("angle", "tile", "slab", None),
        P("angle", "tile", "slab", None),
        P("angle", "tile", "slab"),
        P("angle"),
    )
    out_specs = P(None, "slab", "tile", None)
    return jax.shard_map(
        per_device, mesh=mesh, in_specs=in_specs, out_specs=out_specs, check_vma=False
    )
```

profile of v0, /device:TPU:4, one launch (start us, length us, event | category | flops | bytes accessed | tf_op | source)
XLA Modules:
  0.0 277.0 jit_solution(9299692051527553479)
XLA Ops:
  7.2 3.4 %fusion.118 = bf16[2,192,1536]{2,1,0:T(8,128)(2,1)} fusion(s32[]{:T(128)} %bitcast.5, bf16[1,2,192,1536]{3,2,1,0:T(8,128)(2,1)} %bitcast.162), kind=kLoop, calls=%fused_computation.158 | loop fusion | flops 2359296 | bytes 2359300 | tf_op jit(solution)/shard_map/vmap(jit(_roll_dynamic))/gather | solution.py:36
  10.7 0.0 all-reduce.6.cloned.1.call-update
  10.7 0.0 all-reduce.8.cloned.1.call-start
  10.8 38.6 %all-reduce.6.cloned.1.call-done = bf16[2,192,1536]{2,1,0:T(8,128)(2,1)} async-done(((bf16[2,192,1536]{2,1,0:T(8,128)(2,1)}), bf16[2,192,1536]{2,1,0:T(8,128)(2,1)}) %all-reduce.6.cloned.1.call-update) | async-done | bytes 1179664 | tf_op jit(solution)/shard_map/psum | solution.py:101
  49.3 2.5 collective-permute-start
  51.9 25.4 %collective-permute-done = bf16[2,192,1536]{2,1,0:T(8,128)(2,1)S(1)} collective-permute-done((bf16[2,192,1536]{2,1,0:T(8,128)(2,1)}, bf16[2,192,1536]{2,1,0:T(8,128)(2,1)S(1)}, u32[]{:S(2)}, u32[]{:S(2)}) %collective-permute-start) | collective-permute-done | bytes 1179680 | tf_op jit(solution)/shard_map/ppermute | solution.py:15
  77.3 1.4 pad_maximum_fusion
  78.7 0.0 copy-start
  78.7 0.0 copy-start.2
  78.7 0.0 copy-start.3
  78.7 2.7 broadcast_in_dim.13
  81.5 0.0 copy-done.2
  81.5 34.9 %while.14 = (s32[]{:T(128)}, f32[2,384,1536]{2,1,0:T(8,128)}, s32[]{:T(128)}, s32[2]{0:T(128)S(1)}, s32[2]{0:T(128)S(1)}, /*index=5*/bf16[2,384,1536]{2,1,0:T(8,...) while((s32[]{:T(128)}, f32[2,384,1536]{2,1,0:T(8,128)}, ...), condition=%wide.region_2.3_spmd.clone.clone, body=%wide.region_1.2_spmd.clone.clone.sunk | while | flops 557645824 | bytes 17695004 | solution.py:122
  82.1 0.6 dynamic_slice.37
  84.8 0.7 dynamic_slice.38
  87.5 0.2 dynamic-slice_convert_fusion.2
  87.7 1.0 fusion.185
  88.7 0.1 fusion.186
  88.8 1.1 fusion.187
  89.9 1.1 fusion.188
  91.1 1.1 fusion.190
  92.2 1.1 fusion.191
  93.3 1.1 fusion.192
  94.5 1.1 fusion.189
  95.6 1.1 convolution_add_fusion.6
  96.8 2.1 multiply_convert_fusion.53
  98.9 1.1 fusion.193
  100.1 1.1 fusion.194
  101.2 1.1 fusion.196
  102.3 1.1 fusion.197
  103.5 1.1 fusion.198
  104.6 1.1 fusion.195
  105.8 1.2 convolution_add_fusion.7
  106.9 1.2 fusion.199
  108.2 0.1 fusion.200
  108.2 1.4 maximum_add_fusion.2
  109.6 6.1 %dynamic_update_slice.6 = f32[2,384,1536]{2,1,0:T(8,128)} dynamic-update-slice(f32[2,384,1536]{2,1,0:T(8,128)} %get-tuple-element.287, f32[2,256,256]{2,1,0:T(8,128)S(1)} %maximum_add_fusion.2, s32[]{:T(128)} %constant.108.clone.1..sunk, s32[]{:T(128)S(6)} %select_n.172, s32[]{:T(128)S(6)} %select_n.173) | dynamic-update-slice | bytes 1048580 | tf_op jit(solution)/shard_map/while/body/dynamic_update_slice | solution.py:84
  116.4 1.8 slice.94
  118.2 1.3 collective-permute-start.1
  119.5 50.6 %collective-permute-done.1 = bf16[2,192,1536]{2,1,0:T(8,128)(2,1)S(1)} collective-permute-done((bf16[2,192,1536]{2,1,0:T(8,128)(2,1)S(1)}, bf16[2,192,1536]{2,1,0:T(8,128)(2,1)S(1)}, u32[]{:S(2)}, u32[]{:S(2)}) %collective-permute-start.1) | collective-permute-done | bytes 1179680 | tf_op jit(solution)/shard_map/ppermute | solution.py:15
  170.1 3.1 %add_convert_fusion = bf16[2,192,1536]{2,1,0:T(8,128)(2,1)} fusion(bf16[2,192,1536]{2,1,0:T(8,128)(2,1)S(1)} %collective-permute-done.1, f32[2,384,1536]{2,1,0:T(8,128)} %get-tuple-element.100), kind=kLoop, calls=%fused_computation.154 | loop fusion | flops 1769472 | bytes 4718592 | tf_op jit(solution)/shard_map/convert_element_type | solution.py:127
  173.2 0.0 all-reduce.8.cloned.1.call-update
  173.2 0.0 all-reduce.10.cloned.1.call-start
  173.3 34.6 %all-reduce.8.cloned.1.call-done = bf16[2,192,1536]{2,1,0:T(8,128)(2,1)} async-done(((bf16[2,192,1536]{2,1,0:T(8,128)(2,1)}), bf16[2,192,1536]{2,1,0:T(8,128)(2,1)}) %all-reduce.8.cloned.1.call-update) | async-done | bytes 1179664 | tf_op jit(solution)/shard_map/psum | solution.py:127
  207.9 3.3 %fusion.115 = bf16[2,1,192,1536]{3,2,1,0:T(8,128)(2,1)} fusion(s32[]{:T(128)} %bitcast.8, bf16[2,192,1536]{2,1,0:T(8,128)(2,1)} %all-reduce.8.cloned.1.call-done), kind=kLoop, calls=%fused_computation.155 | loop fusion | flops 2949120 | bytes 2359300 | tf_op jit(solution)/shard_map/convert_element_type | solution.py:131
  211.2 0.0 all-reduce.10.cloned.1.call-update
  211.2 56.2 %all-reduce.10.cloned.1.call-done = bf16[2,1,192,1536]{3,2,1,0:T(8,128)(2,1)} async-done(((bf16[2,1,192,1536]{3,2,1,0:T(8,128)(2,1)}), bf16[2,1,192,1536]{3,2,1,0:T(8,128)(2,1)}) %all-reduce.10.cloned.1.call-update) | async-done | bytes 1179664 | tf_op jit(solution)/shard_map/psum | solution.py:131
  267.4 3.0 %multiply_subtract_fusion = f32[2,1,192,1536]{3,2,1,0:T(8,128)} fusion(bf16[2,1,192,1536]{3,2,1,0:T(8,128)(2,1)} %all-reduce.10.cloned.1.call-done, bf16[2,1,192,1536]{3,2,1,0:T(8,128)(2,1)S(1)} %copy-done.1), kind=kLoop, calls=%fused_computation.152 | loop fusion | flops 2359296 | bytes 4718592 | tf_op jit(solution)/shard_map/sub | solution.py:132
  (5 shorter events, 0.0 us)
Async XLA Ops:
  6.5 42.8 %all-reduce.6.cloned.1.call-start = ((), (), s32[]{:S(2)}) async-start(), calls=%async_computation | async-start | bytes 2359296 | tf_op jit(solution)/shard_map/psum | solution.py:101
  10.7 197.1 %all-reduce.8.cloned.1.call-start = ((), (), s32[]{:S(2)}) async-start(), calls=%async_computation.1 | async-start | bytes 2359296 | tf_op jit(solution)/shard_map/psum | solution.py:127
  49.3 27.9 %collective-permute-start = (bf16[2,192,1536]{2,1,0:T(8,128)(2,1)}, bf16[2,192,1536]{2,1,0:T(8,128)(2,1)S(1)}, u32[]{:S(2)}, u32[]{:S(2)}) collective-permute-start(bf16[2,192,1536]{2,1,0:T(8,128)(2,1)} %all-reduce.6.cloned.1.call-done), channel_id=1, source_target_pairs={{1,0},{3,2},{5,4},{7,6},{9,8},{11,10},{13,12},{15,14},{17,16},{19,... | collective-permute-start | bytes 3538952 | tf_op jit(solution)/shard_map/ppermute | solution.py:15
  78.7 2.8 %copy-start = (f32[2,256,256]{2,1,0:T(8,128)S(1)}, f32[2,256,256]{2,1,0:T(8,128)}, u32[]{:S(2)}) copy-start(f32[2,256,256]{2,1,0:T(8,128)} %param.10) | copy-start | bytes 1572868
  78.7 2.8 copy-start.2
  78.7 2.8 copy-start.3
  118.2 51.9 %collective-permute-start.1 = (bf16[2,192,1536]{2,1,0:T(8,128)(2,1)S(1)}, bf16[2,192,1536]{2,1,0:T(8,128)(2,1)S(1)}, u32[]{:S(2)}, u32[]{:S(2)}) collective-permute-start(bf16[2,192,1536]{2,1,0:T(8,128)(2,1)S(1)} %slice.94), channel_id=1, source_target_pairs={{0,1},{2,3},{4,5},{6,7},{8,9},{10,11},{12,13},{14,15},{16,17},{18,... | collective-permute-start | bytes 3538952 | tf_op jit(solution)/shard_map/ppermute | solution.py:15
  173.2 94.3 %copy-start.1 = (bf16[2,1,192,1536]{3,2,1,0:T(8,128)(2,1)S(1)}, bf16[2,1,192,1536]{3,2,1,0:T(8,128)(2,1)}, u32[]{:S(2)}) copy-start(bf16[2,1,192,1536]{3,2,1,0:T(8,128)(2,1)} %param.9) | copy-start | bytes 3538948
  173.2 94.2 %all-reduce.10.cloned.1.call-start = ((), (), s32[]{:S(2)}) async-start(), calls=%async_computation.2 | async-start | bytes 2359296 | tf_op jit(solution)/shard_map/psum | solution.py:131
Sparse Core Ops, SparseCore 0:
  10.8 38.4 all-reduce.5
  173.3 34.4 all-reduce.7
  211.4 56.0 all-reduce.9
where the time goes:
time: 280 us; the launch traced here: 277 us
  waiting for transfers between devices  205 us (73%)
  matrix products  19.3 us (7%)
  other arithmetic  17 us (6%)
  between operations  13.9 us (5%)
  local copies, waits for them, and re-layouts  12 us (4%)
  loops' own time  5.48 us (2%)
  starting transfers between devices  3.9 us (1%)
    ppermute x2, waiting for transfers between devices, passed_along(): lax.ppermute(value, axis, [(source, source + steps) for source in range(i...  76 us
    psum x1, waiting for transfers between devices, per_device(): lax.psum(layer_gradient.astype(jnp.bfloat16), 'angle').astype(jnp.float32)  56.2 us
    psum x1, waiting for transfers between devices, per_device(): projection = lax.psum(partial_sum.astype(jnp.bfloat16), 'slab')  38.6 us
    psum x1, waiting for transfers between devices, per_device(): lax.psum(tile_gradient.astype(jnp.bfloat16), 'slab').astype(jnp.float32)  34.6 us
    dot_general x16, matrix products, twodot(): jnp.dot(left_matrix, right_matrix, preferred_element_type=jnp.float32)  19.3 us
    dynamic_update_slice x1, local copies, waits for them, and re-layouts, slot_update(): return lax.dynamic_update_slice(buffer, previous + gradient, corner)  6.12 us
  transfers between devices with their start and end apart: 5, of which 5 were waited for; matrix products, arithmetic and copies ran while one was open for 0% of the time, Pallas kernels for 0%

commit v1 on v0

v1 whole, which is shorter than its diff:
```python
import functools

import jax
import jax.numpy as jnp
import numpy as np
from jax import lax
from jax.experimental import pallas as pl
from jax.experimental.pallas import tpu as pltpu
from jax.sharding import PartitionSpec as P

MESH = pl.DeviceIdType.MESH
BF16 = jnp.bfloat16
F32 = jnp.float32
MIB = 1024 * 1024

angle_center = 600
shear_divisor = 64
step_size = 0.03
floor_square = 0.25
row_chunks = 4


def dft_tables(width):
    line = np.arange(width)
    phase = ((line[:, None] * line[None, :]) % width) * (2.0 * np.pi / width)
    scale = width ** (-0.5)
    return (
        jnp.asarray((np.cos(phase) * scale).astype(np.float32), BF16),
        jnp.asarray((-np.sin(phase) * scale).astype(np.float32), BF16),
    )


def wrapped_shift(angle_value, layer, depth, columns):
    sheared = jnp.right_shift((angle_value - angle_center) * (layer - depth // 2), 6)
    rest = lax.rem(sheared, jnp.int32(columns))
    return jnp.where(rest < 0, rest + columns, rest)


def remote(src, dst, send, recv, axis, index):
    return pltpu.make_async_remote_copy(
        src_ref=src, dst_ref=dst, send_sem=send, recv_sem=recv,
        device_id={axis: index}, device_id_type=MESH,
    )


def slab_partners():
    slab = lax.axis_index("slab")
    core = slab % 2
    side = slab // 2
    return core, side, slab + 1 - 2 * core, slab + 2 - 4 * side


def greet(barrier, axis, index, here):
    @pl.when(here)
    def _():
        pl.semaphore_signal(barrier, inc=1, device_id={axis: index}, device_id_type=MESH)


def project_kernel(
    tiles, angles, rolled, ids, ext, all_ids,
    near, half, far, s1, r1, s2, r2, s3, r3, s4, r4, s5, r5, s6, r6, local_sem,
):
    rows = rolled.shape[1]
    size = rows // row_chunks
    core, side, mate, other = slab_partners()
    tile = lax.axis_index("tile")
    angle = lax.axis_index("angle")

    barrier = pltpu.get_barrier_semaphore()
    pl.semaphore_signal(barrier, inc=1, device_id={"slab": mate}, device_id_type=MESH)
    pl.semaphore_signal(barrier, inc=1, device_id={"slab": other}, device_id_type=MESH)
    for step in range(1, angles):
        pl.semaphore_signal(
            barrier, inc=1, device_id={"angle": (angle + step) % angles}, device_id_type=MESH
        )
    greet(barrier, "tile", tile - 1, tile > 0)
    greet(barrier, "tile", tile + 1, tile < tiles - 1)
    peers = (tile > 0).astype(jnp.int32) + (tile < tiles - 1).astype(jnp.int32)
    pl.semaphore_wait(barrier, 1 + angles + peers)

    def part(k, base=0):
        return pl.ds(base + k * size, size)

    first = [
        remote(rolled.at[1 - core, part(k)], near.at[part(k)], s1.at[k], r1.at[k], "slab", mate)
        for k in range(row_chunks)
    ]
    for copy in first:
        copy.start()
    id_copies = [
        remote(ids, all_ids.at[angle], s6.at[step], r6.at[step], "angle", (angle + step) % angles)
        for step in range(1, angles)
    ]
    for copy in id_copies:
        copy.start()
    own_ids = pltpu.make_async_copy(ids, all_ids.at[angle], local_sem)
    own_ids.start()

    second = []
    for k in range(row_chunks):
        first[k].wait_recv()
        half[part(k)] = (
            rolled[core, part(k)].astype(F32) + near[part(k)].astype(F32)
        ).astype(BF16)
        second.append(remote(half.at[part(k)], far.at[part(k)], s2.at[k], r2.at[k], "slab", other))
        second[k].start()

    third, down = [], []
    for k in range(row_chunks):
        second[k].wait_recv()
        ext[core, part(k)] = (half[part(k)].astype(F32) + far[part(k)].astype(F32)).astype(BF16)
        down.append(
            remote(
                ext.at[core, part(k)], ext.at[core, part(k, rows)], s4.at[k], r4.at[k],
                "tile", tile - 1,
            )
        )
        pl.when(tile > 0)(down[k].start)
        third.append(
            remote(
                ext.at[core, part(k)], ext.at[core, part(k)], s3.at[k], r3.at[k], "slab", mate
            )
        )
        third[k].start()

    @pl.when(tile < tiles - 1)
    def _():
        fifth = []
        for k in range(row_chunks):
            down[k].wait_recv()
            fifth.append(
                remote(
                    ext.at[core, part(k, rows)], ext.at[core, part(k, rows)],
                    s5.at[k], r5.at[k], "slab", mate,
                )
            )
            fifth[k].start()
        for copy in fifth:
            copy.wait()

    @pl.when(tile == tiles - 1)
    def _():
        ext[:, pl.ds(rows, rows)] = jnp.zeros((2, rows, ext.shape[2]), BF16)

    for copy in third + id_copies:
        copy.wait()
    own_ids.wait()
    for copy in first + second:
        copy.wait_send()

    @pl.when(tile > 0)
    def _():
        for copy in down:
            copy.wait_send()


def project(rolled, ids, tiles, angles):
    rows, columns = rolled.shape[1:]
    vmem = pl.BlockSpec(memory_space=pltpu.VMEM)
    sems = [pltpu.SemaphoreType.DMA((row_chunks,))] * 10
    sems += [pltpu.SemaphoreType.DMA((angles,))] * 2
    return pl.pallas_call(
        functools.partial(project_kernel, tiles, angles),
        out_shape=(
            jax.ShapeDtypeStruct((2, 2 * rows, columns), BF16),
            jax.ShapeDtypeStruct((angles,) + ids.shape, jnp.int32),
        ),
        in_specs=[vmem, vmem],
        out_specs=(vmem, vmem),
        scratch_shapes=[pltpu.VMEM((rows, columns), BF16)] * 3 + sems + [pltpu.SemaphoreType.DMA],
        compiler_params=pltpu.CompilerParams(
            collective_id=0, has_side_effects=True, vmem_limit_bytes=24 * MIB
        ),
    )(rolled, ids)


def dot(left, right):
    return jnp.dot(left, right, preferred_element_type=F32)


def patch_gradient(phase, absorb, probe_real, probe_imag, pattern, table_real, table_imag):
    mag = jnp.exp(-absorb)
    trans_real = mag * jnp.cos(phase)
    trans_imag = mag * jnp.sin(phase)
    wave_real = (probe_real * trans_real - probe_imag * trans_imag).astype(BF16)
    wave_imag = (probe_real * trans_imag + probe_imag * trans_real).astype(BF16)
    left_real = (dot(table_real, wave_real) - dot(table_imag, wave_imag)).astype(BF16)
    left_imag = (dot(table_real, wave_imag) + dot(table_imag, wave_real)).astype(BF16)
    far_real = dot(left_real, table_real) - dot(left_imag, table_imag)
    far_imag = dot(left_real, table_imag) + dot(left_imag, table_real)
    keeping = 1.0 - pattern * lax.rsqrt(far_real * far_real + far_imag * far_imag + floor_square)
    resid_real = (far_real * keeping).astype(BF16)
    resid_imag = (far_imag * keeping).astype(BF16)
    back_real = (dot(table_real, resid_real) + dot(table_imag, resid_imag)).astype(BF16)
    back_imag = (dot(table_real, resid_imag) - dot(table_imag, resid_real)).astype(BF16)
    exit_real = dot(back_real, table_real) + dot(back_imag, table_imag)
    exit_imag = dot(back_imag, table_real) - dot(back_real, table_imag)
    mixed_real = probe_real * exit_real + probe_imag * exit_imag
    mixed_imag = probe_real * exit_imag - probe_imag * exit_real
    final_real = trans_real * mixed_real + trans_imag * mixed_imag
    final_imag = trans_real * mixed_imag - trans_imag * mixed_real
    return final_imag, -final_real


def slots_kernel(offsets, starts, counts, ext, probe, patterns, tr, ti, out, total):
    width = patterns.shape[-1]
    tall, wide = width + 16, width + 128
    rows, columns = ext.shape[1:]
    total[...] = jnp.zeros_like(total)

    def visit(slot, carry):
        r, q = offsets[slot], starts[slot]
        r0 = pl.multiple_of(jnp.minimum((r // 16) * 16, rows - tall), 16)
        q0 = pl.multiple_of(jnp.minimum((q // 128) * 128, columns - wide), 128)
        dr, dq = r - r0, q - q0
        block = (pl.ds(r0, tall), pl.ds(q0, wide))

        def window(index):
            raw = ext[(index,) + block].astype(F32)
            raw = pltpu.roll(raw, lax.rem(wide - dq, wide), 1)[:, :width]
            return pltpu.roll(raw, lax.rem(tall - dr, tall), 0)[:width]

        grads = patch_gradient(
            window(0), window(1), probe[0], probe[1], patterns[slot].astype(F32), tr[...], ti[...]
        )
        for index in range(2):
            padded = jnp.concatenate([grads[index], jnp.zeros((16, width), F32)], axis=0)
            padded = pltpu.roll(padded, dr, 0)
            padded = jnp.concatenate([padded, jnp.zeros((tall, 128), F32)], axis=1)
            total[(index,) + block] += pltpu.roll(padded, dq, 1)
        return carry

    lax.fori_loop(0, counts[0], visit, 0)
    out[...] = total[...].astype(BF16)


def slots(offsets, starts, counts, ext, probe, patterns, tables):
    smem = pl.BlockSpec(memory_space=pltpu.SMEM)
    vmem = pl.BlockSpec(memory_space=pltpu.VMEM)
    return pl.pallas_call(
        slots_kernel,
        out_shape=jax.ShapeDtypeStruct(ext.shape, BF16),
        in_specs=[smem] * 3 + [vmem] * 5,
        out_specs=vmem,
        scratch_shapes=[pltpu.VMEM(ext.shape, F32)],
        compiler_params=pltpu.CompilerParams(vmem_limit_bytes=32 * MIB),
    )(offsets, starts, counts, ext, probe, patterns, *tables)


def reduce_kernel(
    tiles, angles, buf, planes,
    near, mine, far, spill, above,
    s1, r1, s2, r2, s3, r3, right_sem, left_sem, line_sem, sx, rx, sp, rp, sf, rf,
):
    rows = buf.shape[1] // 2
    part = rows // 2
    core, side, mate, other = slab_partners()
    tile = lax.axis_index("tile")
    angle = lax.axis_index("angle")

    barrier = pltpu.get_barrier_semaphore()
    pl.semaphore_signal(barrier, inc=1, device_id={"slab": mate}, device_id_type=MESH)
    pl.semaphore_signal(barrier, inc=1, device_id={"slab": other}, device_id_type=MESH)
    sides = [
        ("tile", tile - 1, tile > 0), ("tile", tile + 1, tile < tiles - 1),
        ("angle", angle - 1, angle > 0), ("angle", angle + 1, angle < angles - 1),
    ]
    for axis, index, here in sides:
        greet(barrier, axis, index, here)
    pl.semaphore_wait(barrier, 2 + sum(here.astype(jnp.int32) for _, _, here in sides))

    def block(below, half):
        return pl.ds(pl.multiple_of(below * rows + half * part, 16), part)

    blocks = [block(1, 1 - side), block(0, 1 - side), block(1, side), block(0, side)]
    first = [
        remote(buf.at[1 - core, rng], near.at[i], s1.at[i], r1.at[i], "slab", mate)
        for i, rng in enumerate(blocks)
    ]
    for copy in first:
        copy.start()
    second = []
    for i in range(2):
        first[i].wait_recv()
        mine[i] = (buf[core, blocks[i]].astype(F32) + near[i].astype(F32)).astype(BF16)
        second.append(remote(mine.at[i], far.at[i], s2.at[i], r2.at[i], "slab", other))
        second[i].start()

    first[2].wait_recv()
    second[0].wait_recv()
    spill[...] = (
        buf[core, blocks[2]].astype(F32) + near[2].astype(F32) + far[0].astype(F32)
    ).astype(BF16)
    down = remote(spill, above, s3, r3, "tile", tile + 1)
    pl.when(tile < tiles - 1)(down.start)

    @pl.when(tile == 0)
    def _():
        above[...] = jnp.zeros_like(above)

    first[3].wait_recv()
    second[1].wait_recv()
    pl.when(tile > 0)(down.wait_recv)
    planes[angle, core, block(0, side)] = (
        buf[core, blocks[3]].astype(F32) + near[3].astype(F32)
        + far[1].astype(F32) + above[...].astype(F32)
    ).astype(BF16)

    def quarter(origin, half):
        return planes.at[origin, core, block(0, half)]

    def to_right(origin):
        ref = quarter(origin, side)
        return remote(ref, ref, right_sem.at[origin], line_sem.at[origin], "angle", angle + 1)

    def to_left(origin):
        ref = quarter(origin, side)
        return remote(ref, ref, left_sem.at[origin], line_sem.at[origin], "angle", angle - 1)

    def to_other(origin):
        ref = quarter(origin, side)
        return remote(ref, ref, sx.at[origin], rx.at[origin], "slab", other)

    def to_mate(origin):
        ref = quarter(origin, side)
        return remote(ref, ref, sp.at[origin], rp.at[origin], "slab", mate)

    def pass_mate(origin):
        ref = quarter(origin, 1 - side)
        return remote(ref, ref, sf.at[origin], rf.at[origin], "slab", mate)

    def forward(origin):
        to_other(origin).start()
        to_mate(origin).start()

    pl.when(angle < angles - 1)(lambda: to_right(angle).start())
    pl.when(angle > 0)(lambda: to_left(angle).start())
    forward(angle)

    def share(origin):
        to_other(origin).wait_recv()
        pass_mate(origin).start()

    def step_origins(step):
        return [
            (angle - step, angle >= step),
            (angle + step, angle + step <= angles - 1),
        ]

    for step in range(1, angles + 1):
        if step < angles:
            left, right = step_origins(step)

            @pl.when(left[1])
            def _():
                to_right(left[0]).wait_recv()
                pl.when(angle < angles - 1)(lambda: to_right(left[0]).start())
                forward(left[0])

            @pl.when(right[1])
            def _():
                to_left(right[0]).wait_recv()
                pl.when(angle > 0)(lambda: to_left(right[0]).start())
                forward(right[0])

        if step == 1:
            share(angle)
        else:
            for origin, here in step_origins(step - 1):
                pl.when(here)(lambda origin=origin: share(origin))

    for origin in range(angles):
        to_other(origin).wait_send()
        to_mate(origin).wait()
        pass_mate(origin).wait()

        @pl.when((angle < angles - 1) & (origin <= angle))
        def _():
            to_right(origin).wait_send()

        @pl.when((angle > 0) & (origin >= angle))
        def _():
            to_left(origin).wait_send()

    for copy in first + second:
        copy.wait_send()
    pl.when(tile < tiles - 1)(down.wait_send)


def reduce_planes(buf, tiles, angles):
    rows, columns = buf.shape[1] // 2, buf.shape[2]
    part = rows // 2
    vmem = pl.BlockSpec(memory_space=pltpu.VMEM)
    dma = pltpu.SemaphoreType.DMA
    return pl.pallas_call(
        functools.partial(reduce_kernel, tiles, angles),
        out_shape=jax.ShapeDtypeStruct((angles, 2, rows, columns), BF16),
        in_specs=[vmem],
        out_specs=vmem,
        scratch_shapes=[
            pltpu.VMEM((4, part, columns), BF16),
            pltpu.VMEM((2, part, columns), BF16),
            pltpu.VMEM((2, part, columns), BF16),
            pltpu.VMEM((part, columns), BF16),
            pltpu.VMEM((part, columns), BF16),
            dma((4,)), dma((4,)), dma((2,)), dma((2,)), dma, dma,
        ] + [dma((angles,))] * 9,
        compiler_params=pltpu.CompilerParams(
            collective_id=1, has_side_effects=True, vmem_limit_bytes=48 * MIB
        ),
    )(buf)


def update_kernel(depth, ids, volume, planes, out):
    angles, _, _, columns = planes.shape
    layer = lax.axis_index("slab")
    total = jnp.zeros(planes.shape[2:], F32)
    for a in range(angles):
        shift = wrapped_shift(ids[a, 0, 0], layer, depth, columns)
        total += pltpu.roll(planes[a, 0].astype(F32), shift, 1)
    out[0, 0] = volume[0, 0].astype(F32) - step_size * total


def update(ids, volume, planes, depth):
    angles, _, rows, columns = planes.shape
    size = rows // 4
    return pl.pallas_call(
        functools.partial(update_kernel, depth),
        out_shape=jax.ShapeDtypeStruct(volume.shape, F32),
        grid=(2, 4),
        in_specs=[
            pl.BlockSpec(memory_space=pltpu.SMEM),
            pl.BlockSpec((1, 1, size, columns), lambda p, i: (p, 0, i, 0)),
            pl.BlockSpec((angles, 1, size, columns), lambda p, i: (0, p, i, 0)),
        ],
        out_specs=pl.BlockSpec((1, 1, size, columns), lambda p, i: (p, 0, i, 0)),
        compiler_params=pltpu.CompilerParams(vmem_limit_bytes=32 * MIB),
    )(ids, volume, planes)


def per_device(tiles, angles, slabs, volume, probe, amplitudes, offsets, starts, counts, angle_ids):
    columns = volume.shape[3]
    width = amplitudes.shape[-1]
    capacity = offsets.shape[3]
    depth = slabs * volume.shape[1]
    shift = wrapped_shift(angle_ids[0], lax.axis_index("slab"), depth, columns)
    rolled = jnp.roll(volume[:, 0], -shift, axis=-1)
    ids = jnp.broadcast_to(angle_ids[0], (8, 128))
    ext, all_ids = project(rolled, ids, tiles, angles)
    buf = slots(
        offsets.reshape(capacity), starts.reshape(capacity), counts.reshape(1), ext, probe,
        amplitudes.reshape(capacity, width, width), dft_tables(width),
    )
    planes = reduce_planes(buf, tiles, angles)
    return update(all_ids, volume, planes, depth)


def solution(mesh):
    in_specs = (
        P(None, "slab", "tile", None),
        P(),
        P("angle", "tile", "slab", None, None, None),
        P("angle", "tile", "slab", None),
        P("angle", "tile", "slab", None),
        P("angle", "tile", "slab"),
        P("angle"),
    )
    body = functools.partial(
        per_device, mesh.shape["tile"], mesh.shape["angle"], mesh.shape["slab"]
    )
    return jax.shard_map(
        body, mesh=mesh, in_specs=in_specs, out_specs=P(None, "slab", "tile", None),
        check_vma=False,
    )
```

time: 280 us -> 100 us (0.36)
  waiting for transfers between devices: 205 us -> 0 us
  Pallas kernels: 0 us -> 93.3 us
  matrix products: 19.3 us -> 0 us
  other arithmetic: 17 us -> 2.35 us
  between operations: 13.9 us -> 1.55 us
  local copies, waits for them, and re-layouts: 12 us -> 2.36 us
  loops' own time: 5.48 us -> 0 us
  starting transfers between devices: 3.9 us -> 0 us
    psum x3 -> x0, waiting for transfers between devices: 129 us -> none  [the longest x1 56.2 us: per_device(): lax.psum(layer_gradient.astype(jnp.bfloat16), 'angle').astype(jnp.float32)]
    pallas_call x0 -> x4, Pallas kernels: none -> 93.3 us  [the longest x1 59.1 us: reduce_planes(): pl.pallas_call(functools.partial(reduce_kernel, tiles, angles), out_shape...]
    ppermute x2 -> x0, waiting for transfers between devices: 76 us -> none  [passed_along(): lax.ppermute(value, axis, [(source, source + steps) for source in range(i...]
    dot_general x16 -> x0, matrix products: 19.3 us -> none  [twodot(): jnp.dot(left_matrix, right_matrix, preferred_element_type=jnp.float32)]
    convert_element_type x5 -> x0, other arithmetic: 7.7 us -> none  [the longest x1 3.35 us: per_device(): layer_gradient.astype(jnp.bfloat16)]
    dynamic_update_slice x1 -> x0, local copies, waits for them, and re-layouts: 6.12 us -> none  [slot_update(): return lax.dynamic_update_slice(buffer, previous + gradient, corner)]
    another operation x1 -> x0, loops' own time: 5.48 us -> none  [per_device(): buffer = lax.fori_loop(0, own_count[0], visit_own, zero_buffer)]
    ppermute x2 -> x0, starting transfers between devices: 3.81 us -> none  [passed_along(): lax.ppermute(value, axis, [(source, source + steps) for source in range(i...]
  transfers between devices with their start and end apart: 5 -> 0, of which waited for: 5 -> 0; matrix products, arithmetic and copies ran while one was open for 0% -> 0% of each run, Pallas kernels for 0% -> 0%
where the time goes in v1:
time: 100 us; the launch traced here: 99.6 us
  Pallas kernels  93.3 us (93%)
  local copies, waits for them, and re-layouts  2.36 us (2%)
  other arithmetic  2.35 us (2%)
  between operations  1.55 us (2%)
    pallas_call x1, Pallas kernels, reduce_planes(): pl.pallas_call(functools.partial(reduce_kernel, tiles, angles), out_shape...  59.1 us
    pallas_call x1, Pallas kernels, project(): pl.pallas_call(functools.partial(project_kernel, tiles, angles), out_shap...  24.2 us
    pallas_call x1, Pallas kernels, update(): pl.pallas_call(functools.partial(update_kernel, depth), out_shape=jax.Sha...  6.06 us
    pallas_call x1, Pallas kernels, slots(): pl.pallas_call(slots_kernel, out_shape=jax.ShapeDtypeStruct(ext.shape, BF...  3.99 us
    unnamed x16, local copies, waits for them, and re-layouts  2.36 us
    concatenate x1, other arithmetic, per_device(): rolled = jnp.roll(volume[:, 0], -shift, axis=-1)  2.35 us

profile of v1, /device:TPU:4, one launch (start us, length us, event | category | flops | bytes accessed | tf_op | source)
XLA Modules:
  0.0 99.6 jit_solution(14109038004666953558)
XLA Ops:
  0.0 0.0 copy-start.4
  0.0 0.0 copy-start.5
  0.0 0.0 copy-start.7
  0.0 0.0 copy-start.6
  0.0 0.0 copy-start.3
  0.0 0.0 copy-start.2
  1.5 2.4 %fusion.rolled = bf16[2,192,1536]{2,1,0:T(8,128)(2,1)S(1)} fusion(s32[]{:T(128)S(6)} %select_n.18, bf16[2,192,1536]{2,1,0:T(8,128)(2,1)} %bitcast.9), kind=kLoop, calls=%fused_computation.2 | loop fusion | flops 2359296 | bytes 2359300 | tf_op jit(solution)/shard_map/jit(_roll_dynamic)/concatenate | solution.py:447
  3.8 24.2 %shard_map.91 = (bf16[2,384,1536]{2,1,0:T(8,128)(2,1)S(1)}, s32[4,8,128]{2,1,0:T(8,128)S(1)}) custom-call(bf16[2,192,1536]{2,1,0:T(8,128)(2,1)S(1)} %fusion.rolled, s32[8,128]{1,0:T(8,128)S(1)} %broadcast_in_dim.3.ids), custom_call_target="tpu_custom_call" | custom-call | tf_op jit(solution)/shard_map/pallas_call | solution.py:162
  28.0 0.0 copy-done.4
  28.0 0.0 copy-done.5
  28.0 0.0 copy-done.7
  28.0 0.0 copy-done.6
  28.1 0.0 copy-done.3
  28.1 0.0 copy-done.2
  28.1 4.0 %shard_map.92.buf = bf16[2,384,1536]{2,1,0:T(8,128)(2,1)S(1)} custom-call(s32[2]{0:T(128)S(1)} %bitcast.11, s32[2]{0:T(128)S(1)} %bitcast.12, s32[1]{0:T(128)} %bitcast.6.counts, bf16[2,384,1536]{2,1,0:T(8,128)(2,1)S(1)} %get-tuple-element.8.ext, f32[2,256,256]{2,1,0:T(8,128)S(1)} %copy-done.2, bf16[2,256,256]{2,1,0:T(8,128)(2,1)S(1)} %bitcast.10, ...), custom_call_target="tpu_custom_call" | custom-call | tf_op jit(solution)/shard_map/pallas_call | solution.py:240
  32.1 0.0 copy-start.1
  32.1 59.1 %shard_map.93.planes = bf16[4,2,192,1536]{3,2,1,0:T(8,128)(2,1)} custom-call(bf16[2,384,1536]{2,1,0:T(8,128)(2,1)S(1)} %shard_map.92.buf), custom_call_target="tpu_custom_call" | custom-call | tf_op jit(solution)/shard_map/pallas_call | solution.py:395
  91.2 0.0 copy-done.1
  91.2 0.0 copy-start
  91.2 2.3 %copy-done = bf16[4,2,192,1536]{3,2,1,0:T(8,128)(2,1)S(1)} copy-done((bf16[4,2,192,1536]{3,2,1,0:T(8,128)(2,1)S(1)}, bf16[4,2,192,1536]{3,2,1,0:T(8,128)(2,1)}, u32[]{:S(2)}) %copy-start) | copy-done | bytes 4718616
  93.5 6.1 %shard_map.94 = f32[2,1,192,1536]{3,2,1,0:T(8,128)} custom-call(s32[4,8,128]{2,1,0:T(8,128)S(1)} %get-tuple-element.7.ids, bf16[2,1,192,1536]{3,2,1,0:T(8,128)(2,1)S(1)} %copy-done.1, bf16[4,2,192,1536]{3,2,1,0:T(8,128)(2,1)S(1)} %copy-done), custom_call_target="tpu_custom_call" | custom-call | tf_op jit(solution)/shard_map/pallas_call | solution.py:427
  (1 shorter events, 0.0 us)
Async XLA Ops:
  0.0 28.0 %copy-start.4 = (bf16[256,256]{1,0:T(8,128)(2,1)S(1)}, bf16[256,256]{1,0:T(8,128)(2,1)}, u32[]{:S(2)}) copy-start(bf16[256,256]{1,0:T(8,128)(2,1)} %constant.40.clone.ti) | copy-start | bytes 393220
  0.0 28.0 %copy-start.5 = (bf16[256,256]{1,0:T(8,128)(2,1)S(1)}, bf16[256,256]{1,0:T(8,128)(2,1)}, u32[]{:S(2)}) copy-start(bf16[256,256]{1,0:T(8,128)(2,1)} %constant.39.clone.tr) | copy-start | bytes 393220
  0.0 28.0 %copy-start.7 = (s32[1,1,1,2]{3,2,1,0:T(1,128)S(1)}, s32[1,1,1,2]{3,2,1,0:T(1,128)}, u32[]{:S(2)}) copy-start(s32[1,1,1,2]{3,2,1,0:T(1,128)} %param.13) | copy-start | bytes 28
  0.0 28.0 %copy-start.6 = (s32[1,1,1,2]{3,2,1,0:T(1,128)S(1)}, s32[1,1,1,2]{3,2,1,0:T(1,128)}, u32[]{:S(2)}) copy-start(s32[1,1,1,2]{3,2,1,0:T(1,128)} %param.12) | copy-start | bytes 28
  0.0 28.0 %copy-start.3 = (bf16[1,1,1,2,256,256]{5,4,3,2,1,0:T(8,128)(2,1)S(1)}, bf16[1,1,1,2,256,256]{5,4,3,2,1,0:T(8,128)(2,1)}, u32[]{:S(2)}) copy-start(bf16[1,1,1,2,256,256]{5,4,3,2,1,0:T(8,128)(2,1)} %param.11) | copy-start | bytes 786436
  0.0 28.0 %copy-start.2 = (f32[2,256,256]{2,1,0:T(8,128)S(1)}, f32[2,256,256]{2,1,0:T(8,128)}, u32[]{:S(2)}) copy-start(f32[2,256,256]{2,1,0:T(8,128)} %probe.1) | copy-start | bytes 1572868
  32.1 59.1 %copy-start.1 = (bf16[2,1,192,1536]{3,2,1,0:T(8,128)(2,1)S(1)}, bf16[2,1,192,1536]{3,2,1,0:T(8,128)(2,1)}, u32[]{:S(2)}) copy-start(bf16[2,1,192,1536]{3,2,1,0:T(8,128)(2,1)} %volume.1) | copy-start | bytes 3538948
  91.2 2.3 %copy-start = (bf16[4,2,192,1536]{3,2,1,0:T(8,128)(2,1)S(1)}, bf16[4,2,192,1536]{3,2,1,0:T(8,128)(2,1)}, u32[]{:S(2)}) copy-start(bf16[4,2,192,1536]{3,2,1,0:T(8,128)(2,1)} %shard_map.93.planes) | copy-start | bytes 14155780

commit v2 on v1

v2 whole, which is shorter than its diff:
```python
import functools

import jax
import jax.numpy as jnp
import numpy as np
from jax import lax
from jax.experimental import pallas as pl
from jax.experimental.pallas import tpu as pltpu
from jax.sharding import PartitionSpec as P

MESH = pl.DeviceIdType.MESH
BF16 = jnp.bfloat16
F32 = jnp.float32
MIB = 1024 * 1024

angle_center = 600
shear_divisor = 64
step_size = 0.03
floor_square = 0.25
project_rows = 32
reduce_rows = 32


def dft_tables(width):
    line = np.arange(width)
    phase = ((line[:, None] * line[None, :]) % width) * (2.0 * np.pi / width)
    scale = width ** (-0.5)
    return (
        jnp.asarray((np.cos(phase) * scale).astype(np.float32), BF16),
        jnp.asarray((-np.sin(phase) * scale).astype(np.float32), BF16),
    )


def wrapped_shift(angle_value, layer, depth, columns):
    sheared = jnp.right_shift((angle_value - angle_center) * (layer - depth // 2), 6)
    rest = lax.rem(sheared, jnp.int32(columns))
    return jnp.where(rest < 0, rest + columns, rest)


def remote(src, dst, send, recv, axis, index):
    return pltpu.make_async_remote_copy(
        src_ref=src, dst_ref=dst, send_sem=send, recv_sem=recv,
        device_id={axis: index}, device_id_type=MESH,
    )


def slab_partners():
    slab = lax.axis_index("slab")
    core = slab % 2
    side = slab // 2
    return core, side, slab + 1 - 2 * core, slab + 2 - 4 * side


def greet_all(barrier, sides):
    peers = jnp.int32(0)
    for axis, index, here in sides:
        if here is None:
            greet(barrier, axis, index)
            peers += 1
        else:
            pl.when(here)(functools.partial(greet, barrier, axis, index))
            peers += here.astype(jnp.int32)
    pl.semaphore_wait(barrier, peers)


def greet(barrier, axis, index):
    pl.semaphore_signal(barrier, inc=1, device_id={axis: index}, device_id_type=MESH)


def project_kernel(
    tiles, depth, ids, volume, ext,
    send, near, half, far, s1, r1, s2, r2, s3, r3, s4, r4, s5, r5,
):
    rows, columns = volume.shape[2:]
    chunks = rows // project_rows
    core, side, mate, other = slab_partners()
    tile = lax.axis_index("tile")
    shift = wrapped_shift(ids[0], lax.axis_index("slab"), depth, columns)
    back = lax.rem(columns - shift, jnp.int32(columns))

    barrier = pltpu.get_barrier_semaphore()
    sides = [
        ("slab", mate, None), ("slab", other, None),
        ("tile", tile - 1, tile > 0), ("tile", tile + 1, tile < tiles - 1),
    ]
    greet_all(barrier, sides)

    def part(k, base=0):
        return pl.ds(base + k * project_rows, project_rows)

    def rolled(index, k):
        return pltpu.roll(volume[index, 0, part(k)].astype(F32), back, 1)

    first, second, third, down = [], [], [], []
    for k in range(chunks):
        send[part(k)] = rolled(1 - core, k).astype(BF16)
        first.append(
            remote(send.at[part(k)], near.at[part(k)], s1.at[k], r1.at[k], "slab", mate)
        )
        first[k].start()
    for k in range(chunks):
        own = rolled(core, k)
        first[k].wait_recv()
        half[part(k)] = (own + near[part(k)].astype(F32)).astype(BF16)
        second.append(remote(half.at[part(k)], far.at[part(k)], s2.at[k], r2.at[k], "slab", other))
        second[k].start()

    for k in range(chunks):
        second[k].wait_recv()
        ext[core, part(k)] = (half[part(k)].astype(F32) + far[part(k)].astype(F32)).astype(BF16)
        down.append(
            remote(
                ext.at[core, part(k)], ext.at[core, part(k, rows)], s4.at[k], r4.at[k],
                "tile", tile - 1,
            )
        )
        pl.when(tile > 0)(down[k].start)
        third.append(
            remote(
                ext.at[core, part(k)], ext.at[core, part(k)], s3.at[k], r3.at[k], "slab", mate
            )
        )
        third[k].start()

    @pl.when(tile < tiles - 1)
    def _():
        fifth = []
        for k in range(chunks):
            down[k].wait_recv()
            fifth.append(
                remote(
                    ext.at[core, part(k, rows)], ext.at[core, part(k, rows)],
                    s5.at[k], r5.at[k], "slab", mate,
                )
            )
            fifth[k].start()
        for copy in fifth:
            copy.wait()

    @pl.when(tile == tiles - 1)
    def _():
        ext[:, pl.ds(rows, rows)] = jnp.zeros((2, rows, columns), BF16)

    for copy in third:
        copy.wait()
    for copy in first + second:
        copy.wait_send()

    @pl.when(tile > 0)
    def _():
        for copy in down:
            copy.wait_send()


def project(ids, volume, tiles, depth):
    rows, columns = volume.shape[2:]
    vmem = pl.BlockSpec(memory_space=pltpu.VMEM)
    chunks = rows // project_rows
    return pl.pallas_call(
        functools.partial(project_kernel, tiles, depth),
        out_shape=jax.ShapeDtypeStruct((2, 2 * rows, columns), BF16),
        in_specs=[pl.BlockSpec(memory_space=pltpu.SMEM), vmem],
        out_specs=vmem,
        scratch_shapes=[pltpu.VMEM((rows, columns), BF16)] * 4
        + [pltpu.SemaphoreType.DMA((chunks,))] * 10,
        compiler_params=pltpu.CompilerParams(
            collective_id=0, has_side_effects=True, vmem_limit_bytes=24 * MIB
        ),
    )(ids, volume)


def dot(left, right):
    return jnp.dot(left, right, preferred_element_type=F32)


def patch_gradient(phase, absorb, probe_real, probe_imag, pattern, table_real, table_imag):
    mag = jnp.exp(-absorb)
    trans_real = mag * jnp.cos(phase)
    trans_imag = mag * jnp.sin(phase)
    wave_real = (probe_real * trans_real - probe_imag * trans_imag).astype(BF16)
    wave_imag = (probe_real * trans_imag + probe_imag * trans_real).astype(BF16)
    left_real = (dot(table_real, wave_real) - dot(table_imag, wave_imag)).astype(BF16)
    left_imag = (dot(table_real, wave_imag) + dot(table_imag, wave_real)).astype(BF16)
    far_real = dot(left_real, table_real) - dot(left_imag, table_imag)
    far_imag = dot(left_real, table_imag) + dot(left_imag, table_real)
    keeping = 1.0 - pattern * lax.rsqrt(far_real * far_real + far_imag * far_imag + floor_square)
    resid_real = (far_real * keeping).astype(BF16)
    resid_imag = (far_imag * keeping).astype(BF16)
    back_real = (dot(table_real, resid_real) + dot(table_imag, resid_imag)).astype(BF16)
    back_imag = (dot(table_real, resid_imag) - dot(table_imag, resid_real)).astype(BF16)
    exit_real = dot(back_real, table_real) + dot(back_imag, table_imag)
    exit_imag = dot(back_imag, table_real) - dot(back_real, table_imag)
    mixed_real = probe_real * exit_real + probe_imag * exit_imag
    mixed_imag = probe_real * exit_imag - probe_imag * exit_real
    final_real = trans_real * mixed_real + trans_imag * mixed_imag
    final_imag = trans_real * mixed_imag - trans_imag * mixed_real
    return final_imag, -final_real


def slots_kernel(offsets, starts, counts, ext, probe, patterns, tr, ti, out, total):
    width = patterns.shape[-1]
    tall, wide = width + 16, width + 128
    rows, columns = ext.shape[1:]
    total[...] = jnp.zeros_like(total)

    def visit(slot, carry):
        r, q = offsets[slot], starts[slot]
        r0 = pl.multiple_of(jnp.minimum((r // 16) * 16, rows - tall), 16)
        q0 = pl.multiple_of(jnp.minimum((q // 128) * 128, columns - wide), 128)
        dr, dq = r - r0, q - q0
        block = (pl.ds(r0, tall), pl.ds(q0, wide))

        def window(index):
            raw = ext[(index,) + block].astype(F32)
            raw = pltpu.roll(raw, lax.rem(wide - dq, wide), 1)[:, :width]
            return pltpu.roll(raw, lax.rem(tall - dr, tall), 0)[:width]

        grads = patch_gradient(
            window(0), window(1), probe[0], probe[1], patterns[slot].astype(F32), tr[...], ti[...]
        )
        for index in range(2):
            padded = jnp.concatenate([grads[index], jnp.zeros((16, width), F32)], axis=0)
            padded = pltpu.roll(padded, dr, 0)
            padded = jnp.concatenate([padded, jnp.zeros((tall, 128), F32)], axis=1)
            total[(index,) + block] += pltpu.roll(padded, dq, 1)
        return carry

    lax.fori_loop(0, counts[0], visit, 0)
    out[...] = total[...].astype(BF16)


def slots(offsets, starts, counts, ext, probe, patterns, tables):
    smem = pl.BlockSpec(memory_space=pltpu.SMEM)
    vmem = pl.BlockSpec(memory_space=pltpu.VMEM)
    return pl.pallas_call(
        slots_kernel,
        out_shape=jax.ShapeDtypeStruct(ext.shape, BF16),
        in_specs=[smem] * 3 + [vmem] * 5,
        out_specs=vmem,
        scratch_shapes=[pltpu.VMEM(ext.shape, F32)],
        compiler_params=pltpu.CompilerParams(vmem_limit_bytes=32 * MIB),
    )(offsets, starts, counts, ext, probe, patterns, *tables)


def reduce_kernel(
    tiles, angles, depth, ids, volume, buf, out,
    near, near_below, below, above, mine, far, plane, own,
    from_left, from_right, send_right, send_left,
    s1, r1, s2, r2, s3, r3, s4, r4, s5, r5, s6, r6, s7, r7,
):
    rows, columns = volume.shape[2:]
    size = reduce_rows
    chunks = rows // size
    core, side, mate, other = slab_partners()
    tile = lax.axis_index("tile")
    angle = lax.axis_index("angle")
    shift = wrapped_shift(ids[0], lax.axis_index("slab"), depth, columns)
    has_next, has_previous = tile < tiles - 1, tile > 0
    has_right, has_left = angle < angles - 1, angle > 0
    left_is_near = angle < angles // 2

    greet_all(pltpu.get_barrier_semaphore(), [
        ("slab", mate, None), ("slab", other, None),
        ("tile", tile - 1, has_previous), ("tile", tile + 1, has_next),
        ("angle", angle - 1, has_left), ("angle", angle + 1, has_right),
    ])

    def part(k, base=0):
        return pl.ds(base + k * size, size)

    def wide(ref, k):
        return ref[:, part(k)].astype(F32)

    def below_copy(k):
        return remote(
            buf.at[1 - core, part(k, rows)], near_below.at[part(k)], s1.at[k], r1.at[k],
            "slab", mate,
        )

    def near_copy(k):
        return remote(
            buf.at[1 - core, part(k)], near.at[part(k)], s2.at[k], r2.at[k], "slab", mate
        )

    def down_copy(k):
        return remote(below.at[part(k)], above.at[part(k)], s3.at[k], r3.at[k], "tile", tile + 1)

    def far_copy(k):
        return remote(mine.at[part(k)], far.at[part(k)], s4.at[k], r4.at[k], "slab", other)

    def plane_copy(k):
        ref = plane.at[core, part(k)]
        return remote(ref, ref, s5.at[k], r5.at[k], "slab", mate)

    def right_copy(k):
        return remote(
            send_right.at[:, part(k)], from_left.at[:, part(k)], s6.at[k], r6.at[k],
            "angle", angle + 1,
        )

    def left_copy(k):
        return remote(
            send_left.at[:, part(k)], from_right.at[:, part(k)], s7.at[k], r7.at[k],
            "angle", angle - 1,
        )

    for k in range(chunks):
        pl.when(has_next)(lambda k=k: below_copy(k).start())
        near_copy(k).start()

    @pl.when(jnp.logical_not(has_previous))
    def _():
        above[...] = jnp.zeros_like(above)

    @pl.when(jnp.logical_not(has_left))
    def _():
        from_left[...] = jnp.zeros_like(from_left)

    @pl.when(jnp.logical_not(has_right))
    def _():
        from_right[...] = jnp.zeros_like(from_right)

    def pass_below(k):
        below_copy(k).wait_recv()
        below[part(k)] = (
            buf[core, part(k, rows)].astype(F32) + near_below[part(k)].astype(F32)
        ).astype(BF16)
        down_copy(k).start()

    def pair_sum(k):
        near_copy(k).wait_recv()
        pl.when(has_previous)(lambda: down_copy(k).wait_recv())
        mine[part(k)] = (
            buf[core, part(k)].astype(F32)
            + near[part(k)].astype(F32)
            + above[part(k)].astype(F32)
        ).astype(BF16)
        far_copy(k).start()

    def slab_sum(k):
        far_copy(k).wait_recv()
        plane[core, part(k)] = (
            mine[part(k)].astype(F32) + far[part(k)].astype(F32)
        ).astype(BF16)
        plane_copy(k).start()

    def roll_own(k):
        plane_copy(k).wait_recv()
        for index in range(2):
            own[index, part(k)] = pltpu.roll(plane[index, part(k)].astype(F32), shift, 1)

        @pl.when(jnp.logical_not(has_left) & has_right)
        def _():
            send_right[:, part(k)] = own[:, part(k)].astype(BF16)
            right_copy(k).start()

        @pl.when(jnp.logical_not(has_right) & has_left)
        def _():
            send_left[:, part(k)] = own[:, part(k)].astype(BF16)
            left_copy(k).start()

    def move_right(k):
        right_copy(k).wait_recv()

        @pl.when(has_right)
        def _():
            send_right[:, part(k)] = (own[:, part(k)] + wide(from_left, k)).astype(BF16)
            right_copy(k).start()

    def move_left(k):
        left_copy(k).wait_recv()

        @pl.when(has_left)
        def _():
            send_left[:, part(k)] = (own[:, part(k)] + wide(from_right, k)).astype(BF16)
            left_copy(k).start()

    def near_angles(k):
        pl.when(left_is_near & has_left)(lambda: move_right(k))
        pl.when(jnp.logical_not(left_is_near) & has_right)(lambda: move_left(k))

    def far_angles(k):
        pl.when(left_is_near & has_right)(lambda: move_left(k))
        pl.when(jnp.logical_not(left_is_near) & has_left)(lambda: move_right(k))
        total = own[:, part(k)] + wide(from_left, k) + wide(from_right, k)
        out[:, 0, part(k)] = volume[:, 0, part(k)].astype(F32) - step_size * total

    stages = [
        (0, lambda k: pl.when(has_next)(lambda: pass_below(k))),
        (0, pair_sum), (1, slab_sum), (2, roll_own), (3, near_angles), (5, far_angles),
    ]
    for tick in range(chunks + 5):
        for lag, stage in stages:
            if 0 <= tick - lag < chunks:
                stage(tick - lag)

    for k in range(chunks):
        near_copy(k).wait_send()
        far_copy(k).wait_send()
        plane_copy(k).wait_send()

        @pl.when(has_next)
        def _():
            below_copy(k).wait_send()
            down_copy(k).wait_send()

        pl.when(has_right)(lambda: right_copy(k).wait_send())
        pl.when(has_left)(lambda: left_copy(k).wait_send())


def reduce_update(ids, volume, buf, tiles, angles, depth):
    rows, columns = volume.shape[2:]
    vmem = pl.BlockSpec(memory_space=pltpu.VMEM)
    single = pltpu.VMEM((rows, columns), BF16)
    double = pltpu.VMEM((2, rows, columns), BF16)
    return pl.pallas_call(
        functools.partial(reduce_kernel, tiles, angles, depth),
        out_shape=jax.ShapeDtypeStruct(volume.shape, F32),
        in_specs=[pl.BlockSpec(memory_space=pltpu.SMEM), vmem, vmem],
        out_specs=vmem,
        scratch_shapes=[single] * 6
        + [double, pltpu.VMEM((2, rows, columns), F32)]
        + [double] * 4
        + [pltpu.SemaphoreType.DMA((rows // reduce_rows,))] * 14,
        compiler_params=pltpu.CompilerParams(
            collective_id=1, has_side_effects=True, vmem_limit_bytes=40 * MIB
        ),
    )(ids, volume, buf)


def per_device(tiles, angles, slabs, volume, probe, amplitudes, offsets, starts, counts, angle_ids):
    width = amplitudes.shape[-1]
    capacity = offsets.shape[3]
    depth = slabs * volume.shape[1]
    ext = project(angle_ids, volume, tiles, depth)
    buf = slots(
        offsets.reshape(capacity), starts.reshape(capacity), counts.reshape(1), ext, probe,
        amplitudes.reshape(capacity, width, width), dft_tables(width),
    )
    return reduce_update(angle_ids, volume, buf, tiles, angles, depth)


def solution(mesh):
    in_specs = (
        P(None, "slab", "tile", None),
        P(),
        P("angle", "tile", "slab", None, None, None),
        P("angle", "tile", "slab", None),
        P("angle", "tile", "slab", None),
        P("angle", "tile", "slab"),
        P("angle"),
    )
    body = functools.partial(
        per_device, mesh.shape["tile"], mesh.shape["angle"], mesh.shape["slab"]
    )
    return jax.shard_map(
        body, mesh=mesh, in_specs=in_specs, out_specs=P(None, "slab", "tile", None),
        check_vma=False,
    )
```

time: 100 us -> 90.5 us (0.905)
  Pallas kernels: 93.3 us -> 85.6 us
  other arithmetic: 2.35 us -> 0 us
    pallas_call x3 -> x2, Pallas kernels: 89.3 us -> 81.6 us  [the longest x1 61.6 us: reduce_update(): pl.pallas_call(functools.partial(reduce_kernel, tiles, angles, depth), ou...]
    concatenate x1 -> x0, other arithmetic: 2.35 us -> none  [per_device(): rolled = jnp.roll(volume[:, 0], -shift, axis=-1)]
    unnamed x16 -> x17, local copies, waits for them, and re-layouts: 2.36 us -> 2.7 us
where the time goes in v2:
time: 90.5 us; the launch traced here: 89.8 us
  Pallas kernels  85.6 us (95%)
  local copies, waits for them, and re-layouts  2.7 us (3%)
  between operations  1.43 us (2%)
    pallas_call x1, Pallas kernels, reduce_update(): pl.pallas_call(functools.partial(reduce_kernel, tiles, angles, depth), ou...  61.6 us
    pallas_call x1, Pallas kernels, project(): pl.pallas_call(functools.partial(project_kernel, tiles, depth), out_shape...  20 us
    pallas_call x1, Pallas kernels, slots(): pl.pallas_call(slots_kernel, out_shape=jax.ShapeDtypeStruct(ext.shape, BF...  4.02 us
    unnamed x17, local copies, waits for them, and re-layouts  2.7 us

profile of v2, /device:TPU:4, one launch (start us, length us, event | category | flops | bytes accessed | tf_op | source)
XLA Modules:
  0.0 89.8 jit_solution(5092011133682691455)
XLA Ops:
  0.0 0.0 copy-start.7
  0.0 0.0 copy-start.6
  1.3 0.0 copy-start
  1.3 1.3 %copy-done = bf16[2,1,192,1536]{3,2,1,0:T(8,128)(2,1)S(1)} copy-done((bf16[2,1,192,1536]{3,2,1,0:T(8,128)(2,1)S(1)}, bf16[2,1,192,1536]{3,2,1,0:T(8,128)(2,1)}, u32[]{:S(2)}) %copy-start) | copy-done | bytes 1179672
  2.6 0.0 copy-start.2
  2.6 0.0 copy-start.3
  2.6 0.0 copy-start.4
  2.6 0.0 copy-start.5
  2.6 20.0 %shard_map.91.ext = bf16[2,384,1536]{2,1,0:T(8,128)(2,1)S(1)} custom-call(s32[1]{0:T(128)S(6)} %copy.12.ids, bf16[2,1,192,1536]{3,2,1,0:T(8,128)(2,1)S(1)} %copy-done), custom_call_target="tpu_custom_call" | custom-call | tf_op jit(solution)/shard_map/pallas_call | solution.py:159
  22.7 0.0 copy-done.7
  22.7 0.0 copy-done.6
  22.7 0.0 copy-done.2
  22.7 0.0 copy-done.3
  22.7 0.0 copy-done.4
  22.7 0.0 copy-done.5
  22.7 0.0 copy-start.1
  22.7 4.0 %shard_map.92.buf = bf16[2,384,1536]{2,1,0:T(8,128)(2,1)S(1)} custom-call(s32[2]{0:T(128)S(1)} %bitcast.6, s32[2]{0:T(128)S(1)} %bitcast.7, s32[1]{0:T(128)} %bitcast.4.counts, bf16[2,384,1536]{2,1,0:T(8,128)(2,1)S(1)} %shard_map.91.ext, f32[2,256,256]{2,1,0:T(8,128)S(1)} %copy-done.2, bf16[2,256,256]{2,1,0:T(8,128)(2,1)S(1)} %bitcast.5, ...), custom_call_target="tpu_custom_call" | custom-call | tf_op jit(solution)/shard_map/pallas_call | solution.py:235
  26.8 0.0 copy-done.1
  26.8 61.6 %shard_map.93 = f32[2,1,192,1536]{3,2,1,0:T(8,128)S(1)} custom-call(s32[1]{0:T(128)S(6)} %copy.12.ids, bf16[2,1,192,1536]{3,2,1,0:T(8,128)(2,1)S(1)} %copy-done.1, bf16[2,384,1536]{2,1,0:T(8,128)(2,1)S(1)} %shard_map.92.buf), custom_call_target="tpu_custom_call" | custom-call | tf_op jit(solution)/shard_map/pallas_call | solution.py:416
  88.4 1.4 %copy.13 = f32[2,1,192,1536]{3,2,1,0:T(8,128)} copy(f32[2,1,192,1536]{3,2,1,0:T(8,128)S(1)} %shard_map.93) | data formatting | bytes 4718592
Async XLA Ops:
  0.0 22.7 %copy-start.7 = (s32[1,1,1,2]{3,2,1,0:T(1,128)S(1)}, s32[1,1,1,2]{3,2,1,0:T(1,128)}, u32[]{:S(2)}) copy-start(s32[1,1,1,2]{3,2,1,0:T(1,128)} %param.13) | copy-start | bytes 28
  0.0 22.7 %copy-start.6 = (s32[1,1,1,2]{3,2,1,0:T(1,128)S(1)}, s32[1,1,1,2]{3,2,1,0:T(1,128)}, u32[]{:S(2)}) copy-start(s32[1,1,1,2]{3,2,1,0:T(1,128)} %param.12) | copy-start | bytes 28
  1.3 1.3 %copy-start = (bf16[2,1,192,1536]{3,2,1,0:T(8,128)(2,1)S(1)}, bf16[2,1,192,1536]{3,2,1,0:T(8,128)(2,1)}, u32[]{:S(2)}) copy-start(bf16[2,1,192,1536]{3,2,1,0:T(8,128)(2,1)} %volume.3) | copy-start | bytes 3538948
  2.6 20.1 %copy-start.2 = (f32[2,256,256]{2,1,0:T(8,128)S(1)}, f32[2,256,256]{2,1,0:T(8,128)}, u32[]{:S(2)}) copy-start(f32[2,256,256]{2,1,0:T(8,128)} %probe.1) | copy-start | bytes 1572868
  2.6 20.1 %copy-start.3 = (bf16[1,1,1,2,256,256]{5,4,3,2,1,0:T(8,128)(2,1)S(1)}, bf16[1,1,1,2,256,256]{5,4,3,2,1,0:T(8,128)(2,1)}, u32[]{:S(2)}) copy-start(bf16[1,1,1,2,256,256]{5,4,3,2,1,0:T(8,128)(2,1)} %param.11) | copy-start | bytes 786436
  2.6 20.1 %copy-start.4 = (bf16[256,256]{1,0:T(8,128)(2,1)S(1)}, bf16[256,256]{1,0:T(8,128)(2,1)}, u32[]{:S(2)}) copy-start(bf16[256,256]{1,0:T(8,128)(2,1)} %constant.5.clone.ti) | copy-start | bytes 393220
  2.6 20.1 %copy-start.5 = (bf16[256,256]{1,0:T(8,128)(2,1)S(1)}, bf16[256,256]{1,0:T(8,128)(2,1)}, u32[]{:S(2)}) copy-start(bf16[256,256]{1,0:T(8,128)(2,1)} %constant.4.clone.tr) | copy-start | bytes 393220
  22.7 4.0 %copy-start.1 = (bf16[2,1,192,1536]{3,2,1,0:T(8,128)(2,1)S(1)}, bf16[2,1,192,1536]{3,2,1,0:T(8,128)(2,1)}, u32[]{:S(2)}) copy-start(bf16[2,1,192,1536]{3,2,1,0:T(8,128)(2,1)} %volume.3) | copy-start | bytes 3538948

commit v3 on v2

--- a/solution.py
+++ b/solution.py
@@ -17,8 +17,8 @@
 shear_divisor = 64
 step_size = 0.03
 floor_square = 0.25
-project_rows = 32
-reduce_rows = 32
+project_rows = 16
+reduce_rows = 16
 
 
 def dft_tables(width):
@@ -258,6 +258,7 @@
     has_next, has_previous = tile < tiles - 1, tile > 0
     has_right, has_left = angle < angles - 1, angle > 0
     left_is_near = angle < angles // 2
+    inside = has_left & has_right
 
     greet_all(pltpu.get_barrier_semaphore(), [
         ("slab", mate, None), ("slab", other, None),
@@ -387,12 +388,18 @@
 
     stages = [
         (0, lambda k: pl.when(has_next)(lambda: pass_below(k))),
-        (0, pair_sum), (1, slab_sum), (2, roll_own), (3, near_angles), (5, far_angles),
+        (0, pair_sum), (1, slab_sum), (2, roll_own), (3, near_angles),
+        (5, lambda k: pl.when(inside)(lambda: far_angles(k))),
     ]
     for tick in range(chunks + 5):
         for lag, stage in stages:
             if 0 <= tick - lag < chunks:
                 stage(tick - lag)
+
+    @pl.when(jnp.logical_not(inside))
+    def _():
+        for k in range(chunks):
+            far_angles(k)
 
     for k in range(chunks):
         near_copy(k).wait_send()

time: 90.5 us -> 80 us (0.88)
  Pallas kernels: 85.6 us -> 75.7 us
    pallas_call x1, Pallas kernels: 61.6 us -> 52 us  [reduce_update(): pl.pallas_call(functools.partial(reduce_kernel, tiles, angles, depth), ou...]
where the time goes in v3:
time: 80 us; the launch traced here: 79.8 us
  Pallas kernels  75.7 us (95%)
  local copies, waits for them, and re-layouts  2.7 us (3%)
  between operations  1.43 us (2%)
    pallas_call x1, Pallas kernels, reduce_update(): pl.pallas_call(functools.partial(reduce_kernel, tiles, angles, depth), ou...  52 us
    pallas_call x1, Pallas kernels, project(): pl.pallas_call(functools.partial(project_kernel, tiles, depth), out_shape...  19.7 us
    pallas_call x1, Pallas kernels, slots(): pl.pallas_call(slots_kernel, out_shape=jax.ShapeDtypeStruct(ext.shape, BF...  4.02 us
    unnamed x17, local copies, waits for them, and re-layouts  2.7 us

profile of v3, /device:TPU:4, one launch (start us, length us, event | category | flops | bytes accessed | tf_op | source)
XLA Modules:
  0.0 79.8 jit_solution(13299893425986676464)
XLA Ops:
  0.0 0.0 copy-start.7
  0.0 0.0 copy-start.6
  1.3 0.0 copy-start
  1.3 1.3 %copy-done = bf16[2,1,192,1536]{3,2,1,0:T(8,128)(2,1)S(1)} copy-done((bf16[2,1,192,1536]{3,2,1,0:T(8,128)(2,1)S(1)}, bf16[2,1,192,1536]{3,2,1,0:T(8,128)(2,1)}, u32[]{:S(2)}) %copy-start) | copy-done | bytes 1179672
  2.6 0.0 copy-start.2
  2.6 0.0 copy-start.3
  2.6 0.0 copy-start.4
  2.6 0.0 copy-start.5
  2.6 19.7 %shard_map.91.ext = bf16[2,384,1536]{2,1,0:T(8,128)(2,1)S(1)} custom-call(s32[1]{0:T(128)S(6)} %copy.12.ids, bf16[2,1,192,1536]{3,2,1,0:T(8,128)(2,1)S(1)} %copy-done), custom_call_target="tpu_custom_call" | custom-call | tf_op jit(solution)/shard_map/pallas_call | solution.py:159
  22.4 0.0 copy-done.7
  22.4 0.0 copy-done.6
  22.4 0.0 copy-done.2
  22.4 0.0 copy-done.3
  22.4 0.0 copy-done.4
  22.4 0.0 copy-done.5
  22.4 0.0 copy-start.1
  22.4 4.0 %shard_map.92.buf = bf16[2,384,1536]{2,1,0:T(8,128)(2,1)S(1)} custom-call(s32[2]{0:T(128)S(1)} %bitcast.6, s32[2]{0:T(128)S(1)} %bitcast.7, s32[1]{0:T(128)} %bitcast.4.counts, bf16[2,384,1536]{2,1,0:T(8,128)(2,1)S(1)} %shard_map.91.ext, f32[2,256,256]{2,1,0:T(8,128)S(1)} %copy-done.2, bf16[2,256,256]{2,1,0:T(8,128)(2,1)S(1)} %bitcast.5, ...), custom_call_target="tpu_custom_call" | custom-call | tf_op jit(solution)/shard_map/pallas_call | solution.py:235
  26.5 0.0 copy-done.1
  26.5 52.0 %shard_map.93 = f32[2,1,192,1536]{3,2,1,0:T(8,128)S(1)} custom-call(s32[1]{0:T(128)S(6)} %copy.12.ids, bf16[2,1,192,1536]{3,2,1,0:T(8,128)(2,1)S(1)} %copy-done.1, bf16[2,384,1536]{2,1,0:T(8,128)(2,1)S(1)} %shard_map.92.buf), custom_call_target="tpu_custom_call" | custom-call | tf_op jit(solution)/shard_map/pallas_call | solution.py:423
  78.4 1.4 %copy.13 = f32[2,1,192,1536]{3,2,1,0:T(8,128)} copy(f32[2,1,192,1536]{3,2,1,0:T(8,128)S(1)} %shard_map.93) | data formatting | bytes 4718592
Async XLA Ops:
  0.0 22.4 %copy-start.7 = (s32[1,1,1,2]{3,2,1,0:T(1,128)S(1)}, s32[1,1,1,2]{3,2,1,0:T(1,128)}, u32[]{:S(2)}) copy-start(s32[1,1,1,2]{3,2,1,0:T(1,128)} %param.13) | copy-start | bytes 28
  0.0 22.4 %copy-start.6 = (s32[1,1,1,2]{3,2,1,0:T(1,128)S(1)}, s32[1,1,1,2]{3,2,1,0:T(1,128)}, u32[]{:S(2)}) copy-start(s32[1,1,1,2]{3,2,1,0:T(1,128)} %param.12) | copy-start | bytes 28
  1.3 1.3 %copy-start = (bf16[2,1,192,1536]{3,2,1,0:T(8,128)(2,1)S(1)}, bf16[2,1,192,1536]{3,2,1,0:T(8,128)(2,1)}, u32[]{:S(2)}) copy-start(bf16[2,1,192,1536]{3,2,1,0:T(8,128)(2,1)} %volume.3) | copy-start | bytes 3538948
  2.6 19.8 %copy-start.2 = (f32[2,256,256]{2,1,0:T(8,128)S(1)}, f32[2,256,256]{2,1,0:T(8,128)}, u32[]{:S(2)}) copy-start(f32[2,256,256]{2,1,0:T(8,128)} %probe.1) | copy-start | bytes 1572868
  2.6 19.8 %copy-start.3 = (bf16[1,1,1,2,256,256]{5,4,3,2,1,0:T(8,128)(2,1)S(1)}, bf16[1,1,1,2,256,256]{5,4,3,2,1,0:T(8,128)(2,1)}, u32[]{:S(2)}) copy-start(bf16[1,1,1,2,256,256]{5,4,3,2,1,0:T(8,128)(2,1)} %param.11) | copy-start | bytes 786436
  2.6 19.8 %copy-start.4 = (bf16[256,256]{1,0:T(8,128)(2,1)S(1)}, bf16[256,256]{1,0:T(8,128)(2,1)}, u32[]{:S(2)}) copy-start(bf16[256,256]{1,0:T(8,128)(2,1)} %constant.5.clone.ti) | copy-start | bytes 393220
  2.6 19.8 %copy-start.5 = (bf16[256,256]{1,0:T(8,128)(2,1)S(1)}, bf16[256,256]{1,0:T(8,128)(2,1)}, u32[]{:S(2)}) copy-start(bf16[256,256]{1,0:T(8,128)(2,1)} %constant.4.clone.tr) | copy-start | bytes 393220
  22.4 4.0 %copy-start.1 = (bf16[2,1,192,1536]{3,2,1,0:T(8,128)(2,1)S(1)}, bf16[2,1,192,1536]{3,2,1,0:T(8,128)(2,1)}, u32[]{:S(2)}) copy-start(bf16[2,1,192,1536]{3,2,1,0:T(8,128)(2,1)} %volume.3) | copy-start | bytes 3538948

commit v4 on v3

--- a/solution.py
+++ b/solution.py
@@ -68,15 +68,22 @@
 
 
 def project_kernel(
-    tiles, depth, ids, volume, ext,
-    send, near, half, far, s1, r1, s2, r2, s3, r3, s4, r4, s5, r5,
+    tiles, depth, ids, source, ext,
+    volume, send, near, half, far, s1, r1, s2, r2, s3, r3, s4, r4, s5, r5, loads,
 ):
-    rows, columns = volume.shape[2:]
+    rows, columns = source.shape[2:]
     chunks = rows // project_rows
     core, side, mate, other = slab_partners()
     tile = lax.axis_index("tile")
     shift = wrapped_shift(ids[0], lax.axis_index("slab"), depth, columns)
     back = lax.rem(columns - shift, jnp.int32(columns))
+    parts = (1 - core, core)
+    fetched = [
+        pltpu.make_async_copy(source.at[parts[i], 0], volume.at[parts[i]], loads.at[i])
+        for i in range(2)
+    ]
+    for copy in fetched:
+        copy.start()
 
     barrier = pltpu.get_barrier_semaphore()
     sides = [
@@ -89,15 +96,17 @@
         return pl.ds(base + k * project_rows, project_rows)
 
     def rolled(index, k):
-        return pltpu.roll(volume[index, 0, part(k)].astype(F32), back, 1)
+        return pltpu.roll(volume[index, part(k)].astype(F32), back, 1)
 
     first, second, third, down = [], [], [], []
+    fetched[0].wait()
     for k in range(chunks):
         send[part(k)] = rolled(1 - core, k).astype(BF16)
         first.append(
             remote(send.at[part(k)], near.at[part(k)], s1.at[k], r1.at[k], "slab", mate)
         )
         first[k].start()
+    fetched[1].wait()
     for k in range(chunks):
         own = rolled(core, k)
         first[k].wait_recv()
@@ -159,10 +168,14 @@
     return pl.pallas_call(
         functools.partial(project_kernel, tiles, depth),
         out_shape=jax.ShapeDtypeStruct((2, 2 * rows, columns), BF16),
-        in_specs=[pl.BlockSpec(memory_space=pltpu.SMEM), vmem],
+        in_specs=[
+            pl.BlockSpec(memory_space=pltpu.SMEM), pl.BlockSpec(memory_space=pltpu.HBM)
+        ],
         out_specs=vmem,
-        scratch_shapes=[pltpu.VMEM((rows, columns), BF16)] * 4
-        + [pltpu.SemaphoreType.DMA((chunks,))] * 10,
+        scratch_shapes=[pltpu.VMEM((2, rows, columns), BF16)]
+        + [pltpu.VMEM((rows, columns), BF16)] * 4
+        + [pltpu.SemaphoreType.DMA((chunks,))] * 10
+        + [pltpu.SemaphoreType.DMA((2,))],
         compiler_params=pltpu.CompilerParams(
             collective_id=0, has_side_effects=True, vmem_limit_bytes=24 * MIB
         ),
@@ -173,10 +186,30 @@
     return jnp.dot(left, right, preferred_element_type=F32)
 
 
+def sine_cosine(angle):
+    turns = jnp.floor(angle * (2.0 / np.pi) + 0.5)
+    rest = ((angle - turns * 1.5703125) - turns * 4.837512969970703e-4) - turns * 7.5497899548918e-8
+    square = rest * rest
+    sine = rest + rest * square * (
+        -1.0 / 6 + square * (1.0 / 120 + square * (-1.0 / 5040 + square * (1.0 / 362880)))
+    )
+    cosine = 1.0 + square * (
+        -0.5 + square * (1.0 / 24 + square * (-1.0 / 720 + square * (1.0 / 40320)))
+    )
+    quadrant = turns.astype(jnp.int32)
+    odd = (quadrant & 1) != 0
+    found_sine, found_cosine = jnp.where(odd, cosine, sine), jnp.where(odd, sine, cosine)
+    return (
+        jnp.where((quadrant & 2) != 0, -found_sine, found_sine),
+        jnp.where(((quadrant + 1) & 2) != 0, -found_cosine, found_cosine),
+    )
+
+
 def patch_gradient(phase, absorb, probe_real, probe_imag, pattern, table_real, table_imag):
     mag = jnp.exp(-absorb)
-    trans_real = mag * jnp.cos(phase)
-    trans_imag = mag * jnp.sin(phase)
+    sine, cosine = sine_cosine(phase)
+    trans_real = mag * cosine
+    trans_imag = mag * sine
     wave_real = (probe_real * trans_real - probe_imag * trans_imag).astype(BF16)
     wave_imag = (probe_real * trans_imag + probe_imag * trans_real).astype(BF16)
     left_real = (dot(table_real, wave_real) - dot(table_imag, wave_imag)).astype(BF16)
@@ -197,11 +230,11 @@
     return final_imag, -final_real
 
 
-def slots_kernel(offsets, starts, counts, ext, probe, patterns, tr, ti, out, total):
+def slots_kernel(offsets, starts, counts, ext, probe, patterns, tr, ti, out):
     width = patterns.shape[-1]
     tall, wide = width + 16, width + 128
     rows, columns = ext.shape[1:]
-    total[...] = jnp.zeros_like(total)
+    out[...] = jnp.zeros_like(out)
 
     def visit(slot, carry):
         r, q = offsets[slot], starts[slot]
@@ -222,11 +255,11 @@
             padded = jnp.concatenate([grads[index], jnp.zeros((16, width), F32)], axis=0)
             padded = pltpu.roll(padded, dr, 0)
             padded = jnp.concatenate([padded, jnp.zeros((tall, 128), F32)], axis=1)
-            total[(index,) + block] += pltpu.roll(padded, dq, 1)
+            padded = pltpu.roll(padded, dq, 1) + out[(index,) + block].astype(F32)
+            out[(index,) + block] = padded.astype(BF16)
         return carry
 
     lax.fori_loop(0, counts[0], visit, 0)
-    out[...] = total[...].astype(BF16)
 
 
 def slots(offsets, starts, counts, ext, probe, patterns, tables):
@@ -237,7 +270,6 @@
         out_shape=jax.ShapeDtypeStruct(ext.shape, BF16),
         in_specs=[smem] * 3 + [vmem] * 5,
         out_specs=vmem,
-        scratch_shapes=[pltpu.VMEM(ext.shape, F32)],
         compiler_params=pltpu.CompilerParams(vmem_limit_bytes=32 * MIB),
     )(offsets, starts, counts, ext, probe, patterns, *tables)
 
@@ -269,8 +301,10 @@
     def part(k, base=0):
         return pl.ds(base + k * size, size)
 
-    def wide(ref, k):
-        return ref[:, part(k)].astype(F32)
+    parts = (core, 1 - core)
+
+    def wide(ref, k, p):
+        return ref[parts[p], part(k)].astype(F32)
 
     def below_copy(k):
         return remote(
@@ -293,15 +327,17 @@
         ref = plane.at[core, part(k)]
         return remote(ref, ref, s5.at[k], r5.at[k], "slab", mate)
 
-    def right_copy(k):
+    def right_copy(k, p):
+        where = (parts[p], part(k))
         return remote(
-            send_right.at[:, part(k)], from_left.at[:, part(k)], s6.at[k], r6.at[k],
+            send_right.at[where], from_left.at[where], s6.at[p, k], r6.at[p, k],
             "angle", angle + 1,
         )
 
-    def left_copy(k):
+    def left_copy(k, p):
+        where = (parts[p], part(k))
         return remote(
-            send_left.at[:, part(k)], from_right.at[:, part(k)], s7.at[k], r7.at[k],
+            send_left.at[where], from_right.at[where], s7.at[p, k], r7.at[p, k],
             "angle", angle - 1,
         )
 
@@ -344,52 +380,64 @@
             mine[part(k)].astype(F32) + far[part(k)].astype(F32)
         ).astype(BF16)
         plane_copy(k).start()
-
-    def roll_own(k):
+        roll_own(k, 0)
+
+    def mate_sum(k):
         plane_copy(k).wait_recv()
-        for index in range(2):
-            own[index, part(k)] = pltpu.roll(plane[index, part(k)].astype(F32), shift, 1)
+        roll_own(k, 1)
+
+    def roll_own(k, p):
+        where = (parts[p], part(k))
+        own[where] = pltpu.roll(plane[where].astype(F32), shift, 1)
 
         @pl.when(jnp.logical_not(has_left) & has_right)
         def _():
-            send_right[:, part(k)] = own[:, part(k)].astype(BF16)
-            right_copy(k).start()
+            send_right[where] = own[where].astype(BF16)
+            right_copy(k, p).start()
 
         @pl.when(jnp.logical_not(has_right) & has_left)
         def _():
-            send_left[:, part(k)] = own[:, part(k)].astype(BF16)
-            left_copy(k).start()
-
-    def move_right(k):
-        right_copy(k).wait_recv()
+            send_left[where] = own[where].astype(BF16)
+            left_copy(k, p).start()
+
+    def move_right(k, p):
+        where = (parts[p], part(k))
+        right_copy(k, p).wait_recv()
 
         @pl.when(has_right)
         def _():
-            send_right[:, part(k)] = (own[:, part(k)] + wide(from_left, k)).astype(BF16)
-            right_copy(k).start()
-
-    def move_left(k):
-        left_copy(k).wait_recv()
+            send_right[where] = (own[where] + wide(from_left, k, p)).astype(BF16)
+            right_copy(k, p).start()
+
+    def move_left(k, p):
+        where = (parts[p], part(k))
+        left_copy(k, p).wait_recv()
 
         @pl.when(has_left)
         def _():
-            send_left[:, part(k)] = (own[:, part(k)] + wide(from_right, k)).astype(BF16)
-            left_copy(k).start()
-
-    def near_angles(k):
-        pl.when(left_is_near & has_left)(lambda: move_right(k))
-        pl.when(jnp.logical_not(left_is_near) & has_right)(lambda: move_left(k))
-
-    def far_angles(k):
-        pl.when(left_is_near & has_right)(lambda: move_left(k))
-        pl.when(jnp.logical_not(left_is_near) & has_left)(lambda: move_right(k))
-        total = own[:, part(k)] + wide(from_left, k) + wide(from_right, k)
-        out[:, 0, part(k)] = volume[:, 0, part(k)].astype(F32) - step_size * total
+            send_left[where] = (own[where] + wide(from_right, k, p)).astype(BF16)
+            left_copy(k, p).start()
+
+    def near_angles(k, p):
+        pl.when(left_is_near & has_left)(lambda: move_right(k, p))
+        pl.when(jnp.logical_not(left_is_near) & has_right)(lambda: move_left(k, p))
+
+    def far_angles(k, p):
+        pl.when(left_is_near & has_right)(lambda: move_left(k, p))
+        pl.when(jnp.logical_not(left_is_near) & has_left)(lambda: move_right(k, p))
+        total = own[parts[p], part(k)] + wide(from_left, k, p) + wide(from_right, k, p)
+        out[parts[p], 0, part(k)] = (
+            volume[parts[p], 0, part(k)].astype(F32) - step_size * total
+        )
+
+    def inside_far(k, p):
+        pl.when(inside)(lambda: far_angles(k, p))
 
     stages = [
         (0, lambda k: pl.when(has_next)(lambda: pass_below(k))),
-        (0, pair_sum), (1, slab_sum), (2, roll_own), (3, near_angles),
-        (5, lambda k: pl.when(inside)(lambda: far_angles(k))),
+        (0, pair_sum), (1, slab_sum), (2, mate_sum),
+        (2, lambda k: near_angles(k, 0)), (3, lambda k: near_angles(k, 1)),
+        (4, lambda k: inside_far(k, 0)), (5, lambda k: inside_far(k, 1)),
     ]
     for tick in range(chunks + 5):
         for lag, stage in stages:
@@ -399,7 +447,8 @@
     @pl.when(jnp.logical_not(inside))
     def _():
         for k in range(chunks):
-            far_angles(k)
+            far_angles(k, 0)
+            far_angles(k, 1)
 
     for k in range(chunks):
         near_copy(k).wait_send()
@@ -411,8 +460,9 @@
             below_copy(k).wait_send()
             down_copy(k).wait_send()
 
-        pl.when(has_right)(lambda: right_copy(k).wait_send())
-        pl.when(has_left)(lambda: left_copy(k).wait_send())
+        for p in range(2):
+            pl.when(has_right)(lambda: right_copy(k, p).wait_send())
+            pl.when(has_left)(lambda: left_copy(k, p).wait_send())
 
 
 def reduce_update(ids, volume, buf, tiles, angles, depth):
@@ -428,7 +478,8 @@
         scratch_shapes=[single] * 6
         + [double, pltpu.VMEM((2, rows, columns), F32)]
         + [double] * 4
-        + [pltpu.SemaphoreType.DMA((rows // reduce_rows,))] * 14,
+        + [pltpu.SemaphoreType.DMA((rows // reduce_rows,))] * 10
+        + [pltpu.SemaphoreType.DMA((2, rows // reduce_rows))] * 4,
         compiler_params=pltpu.CompilerParams(
             collective_id=1, has_side_effects=True, vmem_limit_bytes=40 * MIB
         ),

time: 80 us -> 78.2 us (0.978)
  Pallas kernels: 75.7 us -> 73.9 us
    pallas_call x1, Pallas kernels: 52 us -> 50.8 us  [reduce_update(): pl.pallas_call(functools.partial(reduce_kernel, tiles, angles, depth), ou...]
    pallas_call x1, Pallas kernels: 4.02 us -> 3.1 us  [slots(): pl.pallas_call(slots_kernel, out_shape=jax.ShapeDtypeStruct(ext.shape, BF...]
where the time goes in v4:
time: 78.2 us; the launch traced here: 78 us
  Pallas kernels  73.9 us (95%)
  local copies, waits for them, and re-layouts  2.7 us (3%)
  between operations  1.43 us (2%)
    pallas_call x1, Pallas kernels, reduce_update(): pl.pallas_call(functools.partial(reduce_kernel, tiles, angles, depth), ou...  50.8 us
    pallas_call x1, Pallas kernels, project(): pl.pallas_call(functools.partial(project_kernel, tiles, depth), out_shape...  20 us
    pallas_call x1, Pallas kernels, slots(): pl.pallas_call(slots_kernel, out_shape=jax.ShapeDtypeStruct(ext.shape, BF...  3.1 us
    unnamed x17, local copies, waits for them, and re-layouts  2.7 us

profile of v4, /device:TPU:4, one launch (start us, length us, event | category | flops | bytes accessed | tf_op | source)
XLA Modules:
  0.0 78.0 jit_solution(11374030043625773627)
XLA Ops:
  0.0 0.0 copy-start.7
  0.0 0.0 copy-start.6
  1.3 0.0 copy-start
  1.3 1.3 %copy-done = bf16[2,1,192,1536]{3,2,1,0:T(8,128)(2,1)S(1)} copy-done((bf16[2,1,192,1536]{3,2,1,0:T(8,128)(2,1)S(1)}, bf16[2,1,192,1536]{3,2,1,0:T(8,128)(2,1)}, u32[]{:S(2)}) %copy-start) | copy-done | bytes 1179672
  2.6 0.0 copy-start.2
  2.6 0.0 copy-start.3
  2.6 0.0 copy-start.4
  2.6 0.0 copy-start.5
  2.6 20.0 %shard_map.91.ext = bf16[2,384,1536]{2,1,0:T(8,128)(2,1)S(1)} custom-call(s32[1]{0:T(128)S(6)} %copy.12.ids, bf16[2,1,192,1536]{3,2,1,0:T(8,128)(2,1)S(1)} %copy-done), custom_call_target="tpu_custom_call" | custom-call | tf_op jit(solution)/shard_map/pallas_call | solution.py:168
  22.6 0.0 copy-done.7
  22.7 0.0 copy-done.6
  22.7 0.0 copy-done.2
  22.7 0.0 copy-done.3
  22.7 0.0 copy-done.4
  22.7 0.0 copy-done.5
  22.7 0.0 copy-start.1
  22.7 3.1 %shard_map.92.buf = bf16[2,384,1536]{2,1,0:T(8,128)(2,1)S(1)} custom-call(s32[2]{0:T(128)S(1)} %bitcast.6, s32[2]{0:T(128)S(1)} %bitcast.7, s32[1]{0:T(128)} %bitcast.4.counts, bf16[2,384,1536]{2,1,0:T(8,128)(2,1)S(1)} %shard_map.91.ext, f32[2,256,256]{2,1,0:T(8,128)S(1)} %copy-done.2, bf16[2,256,256]{2,1,0:T(8,128)(2,1)S(1)} %bitcast.5, ...), custom_call_target="tpu_custom_call" | custom-call | tf_op jit(solution)/shard_map/pallas_call | solution.py:268
  25.8 0.0 copy-done.1
  25.8 50.8 %shard_map.93 = f32[2,1,192,1536]{3,2,1,0:T(8,128)S(1)} custom-call(s32[1]{0:T(128)S(6)} %copy.12.ids, bf16[2,1,192,1536]{3,2,1,0:T(8,128)(2,1)S(1)} %copy-done.1, bf16[2,384,1536]{2,1,0:T(8,128)(2,1)S(1)} %shard_map.92.buf), custom_call_target="tpu_custom_call" | custom-call | tf_op jit(solution)/shard_map/pallas_call | solution.py:473
  76.6 1.4 %copy.13 = f32[2,1,192,1536]{3,2,1,0:T(8,128)} copy(f32[2,1,192,1536]{3,2,1,0:T(8,128)S(1)} %shard_map.93) | data formatting | bytes 4718592
Async XLA Ops:
  0.0 22.6 %copy-start.7 = (s32[1,1,1,2]{3,2,1,0:T(1,128)S(1)}, s32[1,1,1,2]{3,2,1,0:T(1,128)}, u32[]{:S(2)}) copy-start(s32[1,1,1,2]{3,2,1,0:T(1,128)} %param.13) | copy-start | bytes 28
  0.0 22.7 %copy-start.6 = (s32[1,1,1,2]{3,2,1,0:T(1,128)S(1)}, s32[1,1,1,2]{3,2,1,0:T(1,128)}, u32[]{:S(2)}) copy-start(s32[1,1,1,2]{3,2,1,0:T(1,128)} %param.12) | copy-start | bytes 28
  1.3 1.3 %copy-start = (bf16[2,1,192,1536]{3,2,1,0:T(8,128)(2,1)S(1)}, bf16[2,1,192,1536]{3,2,1,0:T(8,128)(2,1)}, u32[]{:S(2)}) copy-start(bf16[2,1,192,1536]{3,2,1,0:T(8,128)(2,1)} %volume.1) | copy-start | bytes 3538948
  2.6 20.1 %copy-start.2 = (f32[2,256,256]{2,1,0:T(8,128)S(1)}, f32[2,256,256]{2,1,0:T(8,128)}, u32[]{:S(2)}) copy-start(f32[2,256,256]{2,1,0:T(8,128)} %probe.1) | copy-start | bytes 1572868
  2.6 20.1 %copy-start.3 = (bf16[1,1,1,2,256,256]{5,4,3,2,1,0:T(8,128)(2,1)S(1)}, bf16[1,1,1,2,256,256]{5,4,3,2,1,0:T(8,128)(2,1)}, u32[]{:S(2)}) copy-start(bf16[1,1,1,2,256,256]{5,4,3,2,1,0:T(8,128)(2,1)} %param.11) | copy-start | bytes 786436
  2.6 20.1 %copy-start.4 = (bf16[256,256]{1,0:T(8,128)(2,1)S(1)}, bf16[256,256]{1,0:T(8,128)(2,1)}, u32[]{:S(2)}) copy-start(bf16[256,256]{1,0:T(8,128)(2,1)} %constant.5.clone.ti) | copy-start | bytes 393220
  2.6 20.1 %copy-start.5 = (bf16[256,256]{1,0:T(8,128)(2,1)S(1)}, bf16[256,256]{1,0:T(8,128)(2,1)}, u32[]{:S(2)}) copy-start(bf16[256,256]{1,0:T(8,128)(2,1)} %constant.4.clone.tr) | copy-start | bytes 393220
  22.7 3.1 %copy-start.1 = (bf16[2,1,192,1536]{3,2,1,0:T(8,128)(2,1)S(1)}, bf16[2,1,192,1536]{3,2,1,0:T(8,128)(2,1)}, u32[]{:S(2)}) copy-start(bf16[2,1,192,1536]{3,2,1,0:T(8,128)(2,1)} %volume.1) | copy-start | bytes 3538948

commit v5 on v4

--- a/solution.py
+++ b/solution.py
@@ -98,73 +98,81 @@
     def rolled(index, k):
         return pltpu.roll(volume[index, part(k)].astype(F32), back, 1)
 
-    first, second, third, down = [], [], [], []
+    def first(k):
+        return remote(send.at[part(k)], near.at[part(k)], s1, r1.at[k], "slab", mate)
+
+    def second(k):
+        return remote(half.at[part(k)], far.at[part(k)], s2, r2.at[k], "slab", other)
+
+    def third(rng):
+        return remote(ext.at[core, rng], ext.at[core, rng], s3, r3, "slab", mate)
+
+    def down(k):
+        return remote(
+            ext.at[core, part(k)], ext.at[core, part(k, rows)], s4, r4.at[k], "tile", tile - 1
+        )
+
+    def fifth(rng):
+        return remote(ext.at[core, rng], ext.at[core, rng], s5, r5, "slab", mate)
+
+    def start_first(k):
+        send[part(k)] = rolled(1 - core, k).astype(BF16)
+        first(k).start()
+
+    def start_second(k):
+        own = rolled(core, k)
+        first(k).wait_recv()
+        half[part(k)] = (own + near[part(k)].astype(F32)).astype(BF16)
+        second(k).start()
+
     fetched[0].wait()
-    for k in range(chunks):
-        send[part(k)] = rolled(1 - core, k).astype(BF16)
-        first.append(
-            remote(send.at[part(k)], near.at[part(k)], s1.at[k], r1.at[k], "slab", mate)
-        )
-        first[k].start()
+    for k in range(2):
+        start_first(k)
     fetched[1].wait()
     for k in range(chunks):
-        own = rolled(core, k)
-        first[k].wait_recv()
-        half[part(k)] = (own + near[part(k)].astype(F32)).astype(BF16)
-        second.append(remote(half.at[part(k)], far.at[part(k)], s2.at[k], r2.at[k], "slab", other))
-        second[k].start()
+        if k + 2 < chunks:
+            start_first(k + 2)
+        start_second(k)
 
     for k in range(chunks):
-        second[k].wait_recv()
+        second(k).wait_recv()
         ext[core, part(k)] = (half[part(k)].astype(F32) + far[part(k)].astype(F32)).astype(BF16)
-        down.append(
-            remote(
-                ext.at[core, part(k)], ext.at[core, part(k, rows)], s4.at[k], r4.at[k],
-                "tile", tile - 1,
-            )
-        )
-        pl.when(tile > 0)(down[k].start)
-        third.append(
-            remote(
-                ext.at[core, part(k)], ext.at[core, part(k)], s3.at[k], r3.at[k], "slab", mate
-            )
-        )
-        third[k].start()
+        pl.when(tile > 0)(lambda: down(k).start())
+        third(part(k)).start()
 
     @pl.when(tile < tiles - 1)
     def _():
-        fifth = []
         for k in range(chunks):
-            down[k].wait_recv()
-            fifth.append(
-                remote(
-                    ext.at[core, part(k, rows)], ext.at[core, part(k, rows)],
-                    s5.at[k], r5.at[k], "slab", mate,
-                )
-            )
-            fifth[k].start()
-        for copy in fifth:
-            copy.wait()
+            down(k).wait_recv()
+            fifth(part(k, rows)).start()
 
     @pl.when(tile == tiles - 1)
     def _():
         ext[:, pl.ds(rows, rows)] = jnp.zeros((2, rows, columns), BF16)
 
-    for copy in third:
-        copy.wait()
-    for copy in first + second:
-        copy.wait_send()
+    everything = pl.ds(0, rows)
+    remote(send, near, s1, r1.at[0], "slab", mate).wait_send()
+    remote(half, far, s2, r2.at[0], "slab", other).wait_send()
+    third(everything).wait_send()
 
     @pl.when(tile > 0)
     def _():
-        for copy in down:
-            copy.wait_send()
+        remote(ext.at[core, everything], far, s4, r4.at[0], "tile", tile - 1).wait_send()
+
+    remote(send, ext.at[1 - core, everything], s1, r3, "slab", mate).wait_recv()
+
+    @pl.when(tile < tiles - 1)
+    def _():
+        below = pl.ds(rows, rows)
+        fifth(below).wait_send()
+        remote(send, ext.at[1 - core, below], s1, r5, "slab", mate).wait_recv()
 
 
 def project(ids, volume, tiles, depth):
     rows, columns = volume.shape[2:]
     vmem = pl.BlockSpec(memory_space=pltpu.VMEM)
-    chunks = rows // project_rows
+    dma = pltpu.SemaphoreType.DMA
+    many = dma((rows // project_rows,))
     return pl.pallas_call(
         functools.partial(project_kernel, tiles, depth),
         out_shape=jax.ShapeDtypeStruct((2, 2 * rows, columns), BF16),
@@ -174,8 +182,8 @@
         out_specs=vmem,
         scratch_shapes=[pltpu.VMEM((2, rows, columns), BF16)]
         + [pltpu.VMEM((rows, columns), BF16)] * 4
-        + [pltpu.SemaphoreType.DMA((chunks,))] * 10
-        + [pltpu.SemaphoreType.DMA((2,))],
+        + [dma, many, dma, many, dma, dma, dma, many, dma, dma]
+        + [dma((2,))],
         compiler_params=pltpu.CompilerParams(
             collective_id=0, has_side_effects=True, vmem_limit_bytes=24 * MIB
         ),
@@ -212,17 +220,24 @@
     trans_imag = mag * sine
     wave_real = (probe_real * trans_real - probe_imag * trans_imag).astype(BF16)
     wave_imag = (probe_real * trans_imag + probe_imag * trans_real).astype(BF16)
-    left_real = (dot(table_real, wave_real) - dot(table_imag, wave_imag)).astype(BF16)
-    left_imag = (dot(table_real, wave_imag) + dot(table_imag, wave_real)).astype(BF16)
-    far_real = dot(left_real, table_real) - dot(left_imag, table_imag)
-    far_imag = dot(left_real, table_imag) + dot(left_imag, table_real)
+    join = functools.partial(jnp.concatenate, axis=0)
+    beside = functools.partial(jnp.concatenate, axis=1)
+    minus_imag = -table_imag
+    rows_forward, columns_forward = beside([table_real, minus_imag]), join([table_real, minus_imag])
+    columns_cross = join([table_imag, table_real])
+    left_real = dot(rows_forward, join([wave_real, wave_imag])).astype(BF16)
+    left_imag = dot(rows_forward, join([wave_imag, -wave_real])).astype(BF16)
+    left = beside([left_real, left_imag])
+    far_real = dot(left, columns_forward)
+    far_imag = dot(left, columns_cross)
     keeping = 1.0 - pattern * lax.rsqrt(far_real * far_real + far_imag * far_imag + floor_square)
     resid_real = (far_real * keeping).astype(BF16)
     resid_imag = (far_imag * keeping).astype(BF16)
-    back_real = (dot(table_real, resid_real) + dot(table_imag, resid_imag)).astype(BF16)
-    back_imag = (dot(table_real, resid_imag) - dot(table_imag, resid_real)).astype(BF16)
-    exit_real = dot(back_real, table_real) + dot(back_imag, table_imag)
-    exit_imag = dot(back_imag, table_real) - dot(back_real, table_imag)
+    rows_back = beside([table_real, table_imag])
+    back_real = dot(rows_back, join([resid_real, resid_imag])).astype(BF16)
+    back_imag = dot(rows_back, join([resid_imag, -resid_real])).astype(BF16)
+    exit_real = dot(beside([back_real, back_imag]), join([table_real, table_imag]))
+    exit_imag = dot(beside([back_imag, back_real]), columns_forward)
     mixed_real = probe_real * exit_real + probe_imag * exit_imag
     mixed_imag = probe_real * exit_imag - probe_imag * exit_real
     final_real = trans_real * mixed_real + trans_imag * mixed_imag
@@ -236,12 +251,14 @@
     rows, columns = ext.shape[1:]
     out[...] = jnp.zeros_like(out)
 
-    def visit(slot, carry):
+    def place(slot):
         r, q = offsets[slot], starts[slot]
         r0 = pl.multiple_of(jnp.minimum((r // 16) * 16, rows - tall), 16)
         q0 = pl.multiple_of(jnp.minimum((q // 128) * 128, columns - wide), 128)
-        dr, dq = r - r0, q - q0
-        block = (pl.ds(r0, tall), pl.ds(q0, wide))
+        return r - r0, q - q0, (pl.ds(r0, tall), pl.ds(q0, wide))
+
+    def slot_gradient(slot):
+        dr, dq, block = place(slot)
 
         def window(index):
             raw = ext[(index,) + block].astype(F32)
@@ -251,15 +268,24 @@
         grads = patch_gradient(
             window(0), window(1), probe[0], probe[1], patterns[slot].astype(F32), tr[...], ti[...]
         )
+        moved = []
         for index in range(2):
             padded = jnp.concatenate([grads[index], jnp.zeros((16, width), F32)], axis=0)
             padded = pltpu.roll(padded, dr, 0)
             padded = jnp.concatenate([padded, jnp.zeros((tall, 128), F32)], axis=1)
-            padded = pltpu.roll(padded, dq, 1) + out[(index,) + block].astype(F32)
-            out[(index,) + block] = padded.astype(BF16)
-        return carry
-
-    lax.fori_loop(0, counts[0], visit, 0)
+            moved.append(pltpu.roll(padded, dq, 1))
+        return moved
+
+    def visit(live):
+        found = [slot_gradient(slot) for slot in range(live)]
+        for slot in range(live):
+            block = place(slot)[2]
+            for index in range(2):
+                padded = found[slot][index] + out[(index,) + block].astype(F32)
+                out[(index,) + block] = padded.astype(BF16)
+
+    for live in range(1, patterns.shape[0] + 1):
+        pl.when(counts[0] == live)(functools.partial(visit, live))
 
 
 def slots(offsets, starts, counts, ext, probe, patterns, tables):
@@ -308,42 +334,45 @@
 
     def below_copy(k):
         return remote(
-            buf.at[1 - core, part(k, rows)], near_below.at[part(k)], s1.at[k], r1.at[k],
+            buf.at[1 - core, part(k, rows)], near_below.at[part(k)], s1, r1.at[k],
             "slab", mate,
         )
 
     def near_copy(k):
         return remote(
-            buf.at[1 - core, part(k)], near.at[part(k)], s2.at[k], r2.at[k], "slab", mate
+            buf.at[1 - core, part(k)], near.at[part(k)], s2, r2.at[k], "slab", mate
         )
 
     def down_copy(k):
-        return remote(below.at[part(k)], above.at[part(k)], s3.at[k], r3.at[k], "tile", tile + 1)
+        return remote(below.at[part(k)], above.at[part(k)], s3, r3.at[k], "tile", tile + 1)
 
     def far_copy(k):
-        return remote(mine.at[part(k)], far.at[part(k)], s4.at[k], r4.at[k], "slab", other)
+        return remote(mine.at[part(k)], far.at[part(k)], s4, r4.at[k], "slab", other)
 
     def plane_copy(k):
         ref = plane.at[core, part(k)]
-        return remote(ref, ref, s5.at[k], r5.at[k], "slab", mate)
+        return remote(ref, ref, s5, r5.at[k], "slab", mate)
 
     def right_copy(k, p):
         where = (parts[p], part(k))
         return remote(
-            send_right.at[where], from_left.at[where], s6.at[p, k], r6.at[p, k],
+            send_right.at[where], from_left.at[where], s6, r6.at[p, k],
             "angle", angle + 1,
         )
 
     def left_copy(k, p):
         where = (parts[p], part(k))
         return remote(
-            send_left.at[where], from_right.at[where], s7.at[p, k], r7.at[p, k],
+            send_left.at[where], from_right.at[where], s7, r7.at[p, k],
             "angle", angle - 1,
         )
 
-    for k in range(chunks):
-        pl.when(has_next)(lambda k=k: below_copy(k).start())
+    def start_near(k):
+        pl.when(has_next)(lambda: below_copy(k).start())
         near_copy(k).start()
+
+    start_near(0)
+    start_near(1)
 
     @pl.when(jnp.logical_not(has_previous))
     def _():
@@ -434,7 +463,7 @@
         pl.when(inside)(lambda: far_angles(k, p))
 
     stages = [
-        (0, lambda k: pl.when(has_next)(lambda: pass_below(k))),
+        (-2, start_near), (0, lambda k: pl.when(has_next)(lambda: pass_below(k))),
         (0, pair_sum), (1, slab_sum), (2, mate_sum),
         (2, lambda k: near_angles(k, 0)), (3, lambda k: near_angles(k, 1)),
         (4, lambda k: inside_far(k, 0)), (5, lambda k: inside_far(k, 1)),
@@ -450,24 +479,32 @@
             far_angles(k, 0)
             far_angles(k, 1)
 
-    for k in range(chunks):
-        near_copy(k).wait_send()
-        far_copy(k).wait_send()
-        plane_copy(k).wait_send()
-
-        @pl.when(has_next)
-        def _():
-            below_copy(k).wait_send()
-            down_copy(k).wait_send()
-
-        for p in range(2):
-            pl.when(has_right)(lambda: right_copy(k, p).wait_send())
-            pl.when(has_left)(lambda: left_copy(k, p).wait_send())
+    everything = pl.ds(0, rows)
+    remote(buf.at[1 - core, everything], near, s2, r2.at[0], "slab", mate).wait_send()
+    remote(mine, far, s4, r4.at[0], "slab", other).wait_send()
+    remote(plane.at[core], plane.at[core], s5, r5.at[0], "slab", mate).wait_send()
+
+    @pl.when(has_next)
+    def _():
+        remote(
+            buf.at[1 - core, pl.ds(rows, rows)], near_below, s1, r1.at[0], "slab", mate
+        ).wait_send()
+        remote(below, above, s3, r3.at[0], "tile", tile + 1).wait_send()
+
+    @pl.when(has_right)
+    def _():
+        remote(send_right, from_left, s6, r6.at[0, 0], "angle", angle + 1).wait_send()
+
+    @pl.when(has_left)
+    def _():
+        remote(send_left, from_right, s7, r7.at[0, 0], "angle", angle - 1).wait_send()
 
 
 def reduce_update(ids, volume, buf, tiles, angles, depth):
     rows, columns = volume.shape[2:]
     vmem = pl.BlockSpec(memory_space=pltpu.VMEM)
+    dma = pltpu.SemaphoreType.DMA
+    many = dma((rows // reduce_rows,))
     single = pltpu.VMEM((rows, columns), BF16)
     double = pltpu.VMEM((2, rows, columns), BF16)
     return pl.pallas_call(
@@ -478,8 +515,8 @@
         scratch_shapes=[single] * 6
         + [double, pltpu.VMEM((2, rows, columns), F32)]
         + [double] * 4
-        + [pltpu.SemaphoreType.DMA((rows // reduce_rows,))] * 10
-        + [pltpu.SemaphoreType.DMA((2, rows // reduce_rows))] * 4,
+        + [dma, many] * 5
+        + [dma, dma((2, rows // reduce_rows))] * 2,
         compiler_params=pltpu.CompilerParams(
             collective_id=1, has_side_effects=True, vmem_limit_bytes=40 * MIB
         ),

time: 78.2 us -> 76.1 us (0.973)
  Pallas kernels: 73.9 us -> 71.9 us
    pallas_call x1, Pallas kernels: 50.8 us -> 49.2 us  [reduce_update(): pl.pallas_call(functools.partial(reduce_kernel, tiles, angles, depth), ou...]
where the time goes in v5:
time: 76.1 us; the launch traced here: 76 us
  Pallas kernels  71.9 us (94%)
  local copies, waits for them, and re-layouts  2.7 us (4%)
  between operations  1.43 us (2%)
    pallas_call x1, Pallas kernels, reduce_update(): pl.pallas_call(functools.partial(reduce_kernel, tiles, angles, depth), ou...  49.2 us
    pallas_call x1, Pallas kernels, project(): pl.pallas_call(functools.partial(project_kernel, tiles, depth), out_shape...  19.8 us
    pallas_call x1, Pallas kernels, slots(): pl.pallas_call(slots_kernel, out_shape=jax.ShapeDtypeStruct(ext.shape, BF...  2.97 us
    unnamed x17, local copies, waits for them, and re-layouts  2.7 us

profile of v5, /device:TPU:4, one launch (start us, length us, event | category | flops | bytes accessed | tf_op | source)
XLA Modules:
  0.0 76.0 jit_solution(2742103415939996909)
XLA Ops:
  0.0 0.0 copy-start.7
  0.0 0.0 copy-start.6
  1.3 0.0 copy-start
  1.3 1.3 %copy-done = bf16[2,1,192,1536]{3,2,1,0:T(8,128)(2,1)S(1)} copy-done((bf16[2,1,192,1536]{3,2,1,0:T(8,128)(2,1)S(1)}, bf16[2,1,192,1536]{3,2,1,0:T(8,128)(2,1)}, u32[]{:S(2)}) %copy-start) | copy-done | bytes 1179672
  2.6 0.0 copy-start.2
  2.6 0.0 copy-start.3
  2.6 0.0 copy-start.4
  2.6 0.0 copy-start.5
  2.6 19.8 %shard_map.91.ext = bf16[2,384,1536]{2,1,0:T(8,128)(2,1)S(1)} custom-call(s32[1]{0:T(128)S(6)} %copy.12.ids, bf16[2,1,192,1536]{3,2,1,0:T(8,128)(2,1)S(1)} %copy-done), custom_call_target="tpu_custom_call" | custom-call | tf_op jit(solution)/shard_map/pallas_call | solution.py:176
  22.4 0.0 copy-done.7
  22.4 0.0 copy-done.6
  22.4 0.0 copy-done.2
  22.4 0.0 copy-done.3
  22.4 0.0 copy-done.4
  22.4 0.0 copy-done.5
  22.5 0.0 copy-start.1
  22.5 3.0 %shard_map.92.buf = bf16[2,384,1536]{2,1,0:T(8,128)(2,1)S(1)} custom-call(s32[2]{0:T(128)S(1)} %bitcast.6, s32[2]{0:T(128)S(1)} %bitcast.7, s32[1]{0:T(128)} %bitcast.4.counts, bf16[2,384,1536]{2,1,0:T(8,128)(2,1)S(1)} %shard_map.91.ext, f32[2,256,256]{2,1,0:T(8,128)S(1)} %copy-done.2, bf16[2,256,256]{2,1,0:T(8,128)(2,1)S(1)} %bitcast.5, ...), custom_call_target="tpu_custom_call" | custom-call | tf_op jit(solution)/shard_map/pallas_call | solution.py:294
  25.4 0.0 copy-done.1
  25.5 49.2 %shard_map.93 = f32[2,1,192,1536]{3,2,1,0:T(8,128)S(1)} custom-call(s32[1]{0:T(128)S(6)} %copy.12.ids, bf16[2,1,192,1536]{3,2,1,0:T(8,128)(2,1)S(1)} %copy-done.1, bf16[2,384,1536]{2,1,0:T(8,128)(2,1)S(1)} %shard_map.92.buf), custom_call_target="tpu_custom_call" | custom-call | tf_op jit(solution)/shard_map/pallas_call | solution.py:510
  74.6 1.4 %copy.13 = f32[2,1,192,1536]{3,2,1,0:T(8,128)} copy(f32[2,1,192,1536]{3,2,1,0:T(8,128)S(1)} %shard_map.93) | data formatting | bytes 4718592
Async XLA Ops:
  0.0 22.4 %copy-start.7 = (s32[1,1,1,2]{3,2,1,0:T(1,128)S(1)}, s32[1,1,1,2]{3,2,1,0:T(1,128)}, u32[]{:S(2)}) copy-start(s32[1,1,1,2]{3,2,1,0:T(1,128)} %param.13) | copy-start | bytes 28
  0.0 22.4 %copy-start.6 = (s32[1,1,1,2]{3,2,1,0:T(1,128)S(1)}, s32[1,1,1,2]{3,2,1,0:T(1,128)}, u32[]{:S(2)}) copy-start(s32[1,1,1,2]{3,2,1,0:T(1,128)} %param.12) | copy-start | bytes 28
  1.3 1.3 %copy-start = (bf16[2,1,192,1536]{3,2,1,0:T(8,128)(2,1)S(1)}, bf16[2,1,192,1536]{3,2,1,0:T(8,128)(2,1)}, u32[]{:S(2)}) copy-start(bf16[2,1,192,1536]{3,2,1,0:T(8,128)(2,1)} %volume.1) | copy-start | bytes 3538948
  2.6 19.8 %copy-start.2 = (f32[2,256,256]{2,1,0:T(8,128)S(1)}, f32[2,256,256]{2,1,0:T(8,128)}, u32[]{:S(2)}) copy-start(f32[2,256,256]{2,1,0:T(8,128)} %probe.1) | copy-start | bytes 1572868
  2.6 19.8 %copy-start.3 = (bf16[1,1,1,2,256,256]{5,4,3,2,1,0:T(8,128)(2,1)S(1)}, bf16[1,1,1,2,256,256]{5,4,3,2,1,0:T(8,128)(2,1)}, u32[]{:S(2)}) copy-start(bf16[1,1,1,2,256,256]{5,4,3,2,1,0:T(8,128)(2,1)} %param.11) | copy-start | bytes 786436
  2.6 19.8 %copy-start.4 = (bf16[256,256]{1,0:T(8,128)(2,1)S(1)}, bf16[256,256]{1,0:T(8,128)(2,1)}, u32[]{:S(2)}) copy-start(bf16[256,256]{1,0:T(8,128)(2,1)} %constant.5.clone.ti) | copy-start | bytes 393220
  2.6 19.8 %copy-start.5 = (bf16[256,256]{1,0:T(8,128)(2,1)S(1)}, bf16[256,256]{1,0:T(8,128)(2,1)}, u32[]{:S(2)}) copy-start(bf16[256,256]{1,0:T(8,128)(2,1)} %constant.4.clone.tr) | copy-start | bytes 393220
  22.5 3.0 %copy-start.1 = (bf16[2,1,192,1536]{3,2,1,0:T(8,128)(2,1)S(1)}, bf16[2,1,192,1536]{3,2,1,0:T(8,128)(2,1)}, u32[]{:S(2)}) copy-start(bf16[2,1,192,1536]{3,2,1,0:T(8,128)(2,1)} %volume.1) | copy-start | bytes 3538948

commit v6 on v5

--- a/solution.py
+++ b/solution.py
@@ -129,16 +129,20 @@
     for k in range(2):
         start_first(k)
     fetched[1].wait()
-    for k in range(chunks):
-        if k + 2 < chunks:
-            start_first(k + 2)
-        start_second(k)
-
-    for k in range(chunks):
+
+    def finish(k):
         second(k).wait_recv()
         ext[core, part(k)] = (half[part(k)].astype(F32) + far[part(k)].astype(F32)).astype(BF16)
         pl.when(tile > 0)(lambda: down(k).start())
         third(part(k)).start()
+
+    for k in range(chunks + 3):
+        if k + 2 < chunks:
+            start_first(k + 2)
+        if k < chunks:
+            start_second(k)
+        if k >= 3:
+            finish(k - 3)
 
     @pl.when(tile < tiles - 1)
     def _():
@@ -463,12 +467,12 @@
         pl.when(inside)(lambda: far_angles(k, p))
 
     stages = [
-        (-2, start_near), (0, lambda k: pl.when(has_next)(lambda: pass_below(k))),
+        (-3, start_near), (-1, lambda k: pl.when(has_next)(lambda: pass_below(k))),
         (0, pair_sum), (1, slab_sum), (2, mate_sum),
         (2, lambda k: near_angles(k, 0)), (3, lambda k: near_angles(k, 1)),
         (4, lambda k: inside_far(k, 0)), (5, lambda k: inside_far(k, 1)),
     ]
-    for tick in range(chunks + 5):
+    for tick in range(-1, chunks + 5):
         for lag, stage in stages:
             if 0 <= tick - lag < chunks:
                 stage(tick - lag)

time: 76.1 us -> 76 us (level)
  no operation moved by 1% of the time
where the time goes in v6:
time: 76 us; the launch traced here: 75.8 us
  Pallas kernels  71.7 us (94%)
  local copies, waits for them, and re-layouts  2.7 us (4%)
  between operations  1.43 us (2%)
    pallas_call x1, Pallas kernels, reduce_update(): pl.pallas_call(functools.partial(reduce_kernel, tiles, angles, depth), ou...  49.4 us
    pallas_call x1, Pallas kernels, project(): pl.pallas_call(functools.partial(project_kernel, tiles, depth), out_shape...  19.3 us
    pallas_call x1, Pallas kernels, slots(): pl.pallas_call(slots_kernel, out_shape=jax.ShapeDtypeStruct(ext.shape, BF...  2.97 us
    unnamed x17, local copies, waits for them, and re-layouts  2.7 us

profile of v6, /device:TPU:4, one launch (start us, length us, event | category | flops | bytes accessed | tf_op | source)
XLA Modules:
  0.0 75.8 jit_solution(8666169225550505171)
XLA Ops:
  0.0 0.0 copy-start.7
  0.0 0.0 copy-start.6
  1.3 0.0 copy-start
  1.3 1.3 %copy-done = bf16[2,1,192,1536]{3,2,1,0:T(8,128)(2,1)S(1)} copy-done((bf16[2,1,192,1536]{3,2,1,0:T(8,128)(2,1)S(1)}, bf16[2,1,192,1536]{3,2,1,0:T(8,128)(2,1)}, u32[]{:S(2)}) %copy-start) | copy-done | bytes 1179672
  2.6 0.0 copy-start.2
  2.6 0.0 copy-start.3
  2.6 0.0 copy-start.4
  2.6 0.0 copy-start.5
  2.6 19.3 %shard_map.91.ext = bf16[2,384,1536]{2,1,0:T(8,128)(2,1)S(1)} custom-call(s32[1]{0:T(128)S(6)} %copy.12.ids, bf16[2,1,192,1536]{3,2,1,0:T(8,128)(2,1)S(1)} %copy-done), custom_call_target="tpu_custom_call" | custom-call | tf_op jit(solution)/shard_map/pallas_call | solution.py:180
  22.0 0.0 copy-done.7
  22.0 0.0 copy-done.6
  22.0 0.0 copy-done.2
  22.0 0.0 copy-done.3
  22.0 0.0 copy-done.4
  22.0 0.0 copy-done.5
  22.0 0.0 copy-start.1
  22.0 3.0 %shard_map.92.buf = bf16[2,384,1536]{2,1,0:T(8,128)(2,1)S(1)} custom-call(s32[2]{0:T(128)S(1)} %bitcast.6, s32[2]{0:T(128)S(1)} %bitcast.7, s32[1]{0:T(128)} %bitcast.4.counts, bf16[2,384,1536]{2,1,0:T(8,128)(2,1)S(1)} %shard_map.91.ext, f32[2,256,256]{2,1,0:T(8,128)S(1)} %copy-done.2, bf16[2,256,256]{2,1,0:T(8,128)(2,1)S(1)} %bitcast.5, ...), custom_call_target="tpu_custom_call" | custom-call | tf_op jit(solution)/shard_map/pallas_call | solution.py:298
  25.0 0.0 copy-done.1
  25.0 49.4 %shard_map.93 = f32[2,1,192,1536]{3,2,1,0:T(8,128)S(1)} custom-call(s32[1]{0:T(128)S(6)} %copy.12.ids, bf16[2,1,192,1536]{3,2,1,0:T(8,128)(2,1)S(1)} %copy-done.1, bf16[2,384,1536]{2,1,0:T(8,128)(2,1)S(1)} %shard_map.92.buf), custom_call_target="tpu_custom_call" | custom-call | tf_op jit(solution)/shard_map/pallas_call | solution.py:514
  74.4 1.4 %copy.13 = f32[2,1,192,1536]{3,2,1,0:T(8,128)} copy(f32[2,1,192,1536]{3,2,1,0:T(8,128)S(1)} %shard_map.93) | data formatting | bytes 4718592
Async XLA Ops:
  0.0 22.0 %copy-start.7 = (s32[1,1,1,2]{3,2,1,0:T(1,128)S(1)}, s32[1,1,1,2]{3,2,1,0:T(1,128)}, u32[]{:S(2)}) copy-start(s32[1,1,1,2]{3,2,1,0:T(1,128)} %param.13) | copy-start | bytes 28
  0.0 22.0 %copy-start.6 = (s32[1,1,1,2]{3,2,1,0:T(1,128)S(1)}, s32[1,1,1,2]{3,2,1,0:T(1,128)}, u32[]{:S(2)}) copy-start(s32[1,1,1,2]{3,2,1,0:T(1,128)} %param.12) | copy-start | bytes 28
  1.3 1.3 %copy-start = (bf16[2,1,192,1536]{3,2,1,0:T(8,128)(2,1)S(1)}, bf16[2,1,192,1536]{3,2,1,0:T(8,128)(2,1)}, u32[]{:S(2)}) copy-start(bf16[2,1,192,1536]{3,2,1,0:T(8,128)(2,1)} %volume.1) | copy-start | bytes 3538948
  2.6 19.4 %copy-start.2 = (f32[2,256,256]{2,1,0:T(8,128)S(1)}, f32[2,256,256]{2,1,0:T(8,128)}, u32[]{:S(2)}) copy-start(f32[2,256,256]{2,1,0:T(8,128)} %probe.1) | copy-start | bytes 1572868
  2.6 19.4 %copy-start.3 = (bf16[1,1,1,2,256,256]{5,4,3,2,1,0:T(8,128)(2,1)S(1)}, bf16[1,1,1,2,256,256]{5,4,3,2,1,0:T(8,128)(2,1)}, u32[]{:S(2)}) copy-start(bf16[1,1,1,2,256,256]{5,4,3,2,1,0:T(8,128)(2,1)} %param.11) | copy-start | bytes 786436
  2.6 19.4 %copy-start.4 = (bf16[256,256]{1,0:T(8,128)(2,1)S(1)}, bf16[256,256]{1,0:T(8,128)(2,1)}, u32[]{:S(2)}) copy-start(bf16[256,256]{1,0:T(8,128)(2,1)} %constant.5.clone.ti) | copy-start | bytes 393220
  2.6 19.4 %copy-start.5 = (bf16[256,256]{1,0:T(8,128)(2,1)S(1)}, bf16[256,256]{1,0:T(8,128)(2,1)}, u32[]{:S(2)}) copy-start(bf16[256,256]{1,0:T(8,128)(2,1)} %constant.4.clone.tr) | copy-start | bytes 393220
  22.0 3.0 %copy-start.1 = (bf16[2,1,192,1536]{3,2,1,0:T(8,128)(2,1)S(1)}, bf16[2,1,192,1536]{3,2,1,0:T(8,128)(2,1)}, u32[]{:S(2)}) copy-start(bf16[2,1,192,1536]{3,2,1,0:T(8,128)(2,1)} %volume.1) | copy-start | bytes 3538948

commit v7 on v6

--- a/solution.py
+++ b/solution.py
@@ -470,9 +470,9 @@
         (-3, start_near), (-1, lambda k: pl.when(has_next)(lambda: pass_below(k))),
         (0, pair_sum), (1, slab_sum), (2, mate_sum),
         (2, lambda k: near_angles(k, 0)), (3, lambda k: near_angles(k, 1)),
-        (4, lambda k: inside_far(k, 0)), (5, lambda k: inside_far(k, 1)),
+        (3, lambda k: inside_far(k, 0)), (4, lambda k: inside_far(k, 1)),
     ]
-    for tick in range(-1, chunks + 5):
+    for tick in range(-1, chunks + 4):
         for lag, stage in stages:
             if 0 <= tick - lag < chunks:
                 stage(tick - lag)

time: 76 us -> 79.9 us (1.051)
  Pallas kernels: 71.7 us -> 75.6 us
    pallas_call x1, Pallas kernels: 49.4 us -> 53.3 us  [reduce_update(): pl.pallas_call(functools.partial(reduce_kernel, tiles, angles, depth), ou...]
where the time goes in v7:
time: 79.9 us; the launch traced here: 79.7 us
  Pallas kernels  75.6 us (95%)
  local copies, waits for them, and re-layouts  2.7 us (3%)
  between operations  1.43 us (2%)
    pallas_call x1, Pallas kernels, reduce_update(): pl.pallas_call(functools.partial(reduce_kernel, tiles, angles, depth), ou...  53.3 us
    pallas_call x1, Pallas kernels, project(): pl.pallas_call(functools.partial(project_kernel, tiles, depth), out_shape...  19.3 us
    pallas_call x1, Pallas kernels, slots(): pl.pallas_call(slots_kernel, out_shape=jax.ShapeDtypeStruct(ext.shape, BF...  2.97 us
    unnamed x17, local copies, waits for them, and re-layouts  2.7 us

profile of v7, /device:TPU:4, one launch (start us, length us, event | category | flops | bytes accessed | tf_op | source)
XLA Modules:
  0.0 79.7 jit_solution(6243865244029935706)
XLA Ops:
  0.0 0.0 copy-start.7
  0.0 0.0 copy-start.6
  1.3 0.0 copy-start
  1.3 1.3 %copy-done = bf16[2,1,192,1536]{3,2,1,0:T(8,128)(2,1)S(1)} copy-done((bf16[2,1,192,1536]{3,2,1,0:T(8,128)(2,1)S(1)}, bf16[2,1,192,1536]{3,2,1,0:T(8,128)(2,1)}, u32[]{:S(2)}) %copy-start) | copy-done | bytes 1179672
  2.6 0.0 copy-start.2
  2.6 0.0 copy-start.3
  2.6 0.0 copy-start.4
  2.6 0.0 copy-start.5
  2.6 19.3 %shard_map.91.ext = bf16[2,384,1536]{2,1,0:T(8,128)(2,1)S(1)} custom-call(s32[1]{0:T(128)S(6)} %copy.12.ids, bf16[2,1,192,1536]{3,2,1,0:T(8,128)(2,1)S(1)} %copy-done), custom_call_target="tpu_custom_call" | custom-call | tf_op jit(solution)/shard_map/pallas_call | solution.py:180
  22.0 0.0 copy-done.7
  22.0 0.0 copy-done.6
  22.0 0.0 copy-done.2
  22.0 0.0 copy-done.3
  22.0 0.0 copy-done.4
  22.0 0.0 copy-done.5
  22.0 0.0 copy-start.1
  22.0 3.0 %shard_map.92.buf = bf16[2,384,1536]{2,1,0:T(8,128)(2,1)S(1)} custom-call(s32[2]{0:T(128)S(1)} %bitcast.6, s32[2]{0:T(128)S(1)} %bitcast.7, s32[1]{0:T(128)} %bitcast.4.counts, bf16[2,384,1536]{2,1,0:T(8,128)(2,1)S(1)} %shard_map.91.ext, f32[2,256,256]{2,1,0:T(8,128)S(1)} %copy-done.2, bf16[2,256,256]{2,1,0:T(8,128)(2,1)S(1)} %bitcast.5, ...), custom_call_target="tpu_custom_call" | custom-call | tf_op jit(solution)/shard_map/pallas_call | solution.py:298
  25.0 0.0 copy-done.1
  25.0 53.3 %shard_map.93 = f32[2,1,192,1536]{3,2,1,0:T(8,128)S(1)} custom-call(s32[1]{0:T(128)S(6)} %copy.12.ids, bf16[2,1,192,1536]{3,2,1,0:T(8,128)(2,1)S(1)} %copy-done.1, bf16[2,384,1536]{2,1,0:T(8,128)(2,1)S(1)} %shard_map.92.buf), custom_call_target="tpu_custom_call" | custom-call | tf_op jit(solution)/shard_map/pallas_call | solution.py:514
  78.3 1.4 %copy.13 = f32[2,1,192,1536]{3,2,1,0:T(8,128)} copy(f32[2,1,192,1536]{3,2,1,0:T(8,128)S(1)} %shard_map.93) | data formatting | bytes 4718592
Async XLA Ops:
  0.0 22.0 %copy-start.7 = (s32[1,1,1,2]{3,2,1,0:T(1,128)S(1)}, s32[1,1,1,2]{3,2,1,0:T(1,128)}, u32[]{:S(2)}) copy-start(s32[1,1,1,2]{3,2,1,0:T(1,128)} %param.13) | copy-start | bytes 28
  0.0 22.0 %copy-start.6 = (s32[1,1,1,2]{3,2,1,0:T(1,128)S(1)}, s32[1,1,1,2]{3,2,1,0:T(1,128)}, u32[]{:S(2)}) copy-start(s32[1,1,1,2]{3,2,1,0:T(1,128)} %param.12) | copy-start | bytes 28
  1.3 1.3 %copy-start = (bf16[2,1,192,1536]{3,2,1,0:T(8,128)(2,1)S(1)}, bf16[2,1,192,1536]{3,2,1,0:T(8,128)(2,1)}, u32[]{:S(2)}) copy-start(bf16[2,1,192,1536]{3,2,1,0:T(8,128)(2,1)} %volume.1) | copy-start | bytes 3538948
  2.6 19.4 %copy-start.2 = (f32[2,256,256]{2,1,0:T(8,128)S(1)}, f32[2,256,256]{2,1,0:T(8,128)}, u32[]{:S(2)}) copy-start(f32[2,256,256]{2,1,0:T(8,128)} %probe.1) | copy-start | bytes 1572868
  2.6 19.4 %copy-start.3 = (bf16[1,1,1,2,256,256]{5,4,3,2,1,0:T(8,128)(2,1)S(1)}, bf16[1,1,1,2,256,256]{5,4,3,2,1,0:T(8,128)(2,1)}, u32[]{:S(2)}) copy-start(bf16[1,1,1,2,256,256]{5,4,3,2,1,0:T(8,128)(2,1)} %param.11) | copy-start | bytes 786436
  2.6 19.4 %copy-start.4 = (bf16[256,256]{1,0:T(8,128)(2,1)S(1)}, bf16[256,256]{1,0:T(8,128)(2,1)}, u32[]{:S(2)}) copy-start(bf16[256,256]{1,0:T(8,128)(2,1)} %constant.5.clone.ti) | copy-start | bytes 393220
  2.6 19.4 %copy-start.5 = (bf16[256,256]{1,0:T(8,128)(2,1)S(1)}, bf16[256,256]{1,0:T(8,128)(2,1)}, u32[]{:S(2)}) copy-start(bf16[256,256]{1,0:T(8,128)(2,1)} %constant.4.clone.tr) | copy-start | bytes 393220
  22.0 3.0 %copy-start.1 = (bf16[2,1,192,1536]{3,2,1,0:T(8,128)(2,1)S(1)}, bf16[2,1,192,1536]{3,2,1,0:T(8,128)(2,1)}, u32[]{:S(2)}) copy-start(bf16[2,1,192,1536]{3,2,1,0:T(8,128)(2,1)} %volume.1) | copy-start | bytes 3538948
